TPU v7x, 128 devices: a whole 4x4x4 slice. The times are simulated.
128 devices in a mesh: dp: 16 (over x, y), ep: 8 (over z, core).
Axes of the slice: x: 4, y: 4, z: 4, core: 2. Of those that a mesh axis runs over, the one named last changes fastest.
Arguments:
- tokens: bfloat16 [32, 1024, 1024], P('dp', 'ep'), may hold values from -6 to 6
- cotangent: bfloat16 [32, 1024, 1024], P('dp', 'ep'), may hold values from -6 to 6
- block_ids: int32 [32, 1024], P('dp'), may hold values from 0 to 7, never falling along the last dimension, each value on 1 to 256 neighbouring positions
- routes: int32 [32, 1024, 8], P('dp', 'ep'), may hold values from 0 to 31, all different within a row
- w_query: bfloat16 [1024, 1024], P(('dp', 'ep')), may hold values from -0.75 to 0.75
- w_key: bfloat16 [1024, 512], P(('dp', 'ep')), may hold values from -0.75 to 0.75
- w_value: bfloat16 [1024, 512], P(('dp', 'ep')), may hold values from -0.1875 to 0.1875
- w_output: bfloat16 [1024, 1024], P(('dp', 'ep')), may hold values from -3 to 3
- w_router: bfloat16 [1024, 32], P(('dp', 'ep')), may hold values from -0.09375 to 0.09375
- gain_attn: bfloat16 [1024], P(('dp', 'ep')), may hold values from 0.5 to 1.5
- gain_moe: bfloat16 [1024], P(('dp', 'ep')), may hold values from 0.5 to 1.5
- expert_gate: bfloat16 [32, 1024, 512], P('ep'), may hold values from -0.1875 to 0.1875
- expert_up: bfloat16 [32, 1024, 512], P('ep'), may hold values from -0.1875 to 0.1875
- expert_down: bfloat16 [32, 512, 1024], P('ep'), may hold values from -2 to 2
Outputs:
- output: bfloat16 [32, 1024, 1024], P('dp', 'ep')
- grad_tokens: bfloat16 [32, 1024, 1024], P('dp', 'ep')
- grad_query: float32 [1024, 1024], P(('dp', 'ep'))
- grad_key: float32 [1024, 512], P(('dp', 'ep'))
- grad_value: float32 [1024, 512], P(('dp', 'ep'))
- grad_output: float32 [1024, 1024], P(('dp', 'ep'))
- grad_router: float32 [1024, 32], P(('dp', 'ep'))
- grad_gain_attn: float32 [1024], P(('dp', 'ep'))
- grad_gain_moe: float32 [1024], P(('dp', 'ep'))
- grad_expert_gate: float32 [32, 1024, 512], P('ep')
- grad_expert_up: float32 [32, 1024, 512], P('ep')
- grad_expert_down: float32 [32, 512, 1024], P('ep')
Inputs may be any that keep to these rules, and one draw needn't show every extreme that they name: `block_ids`: along each sequence the ids never fall; every id up to the largest occurs on 1 to 256 consecutive tokens, one block has exactly 256. `routes`: each token names 8 different experts; every expert is named by some token.
All inputs are finite; a program needn't handle non-finite values.
Results may differ from a plain program's by a relative error of at most 0.018.
Values may be sent and summed in bfloat16 or wider, within the bound.
A program may use at most 256 MiB of HBM per device.

v0:
```python
import math

import jax
import jax.numpy as jnp
from jax import lax
from jax.sharding import PartitionSpec as P

HEADS = 16
KV_HEADS = 8
HD = 64


epsilon = 1e-06
residual_scale = 0.22
score_scale = 0.015625
rope_base = 10000.0
masked_value = -1e30


def sent_together(arrays, axis, dim, along):
    widths = [math.prod(a.shape[along:]) for a in arrays]
    both = jnp.concatenate(
        [a.reshape(*a.shape[:along], w) for a, w in zip(arrays, widths)], axis=along
    )
    out = lax.all_gather(both, axis, axis=dim, tiled=True)
    blocks = jnp.split(out, [sum(widths[:k]) for k in range(1, len(widths))], axis=along)
    return tuple((b.reshape(*out.shape[:along], *a.shape[along:]) for a, b in zip(arrays, blocks)))


def sent_together_2(arrays, axis, dim, along):
    ends, at = ([], 0)
    for a in arrays[:-1]:
        at += a.shape[along]
        ends.append(at)
    both = jnp.concatenate(arrays, axis=along)
    return tuple(jnp.split(lax.all_gather(both, axis, axis=dim, tiled=True), ends, axis=along))


def in_one_piece(arrays, axis, dim, along):
    widths = [a.shape[along] for a in arrays]
    both = jnp.concatenate(arrays, axis=along)
    out = lax.psum_scatter(both, axis, scatter_dimension=dim, tiled=True)
    return tuple(jnp.split(out, [sum(widths[:k]) for k in range(1, len(widths))], axis=along))


def in_blocks(x, dim, length):
    shape = x.shape
    blocks = x.reshape(*shape[:dim], length, shape[dim] // length, *shape[dim + 1 :])
    return jnp.moveaxis(blocks, dim, 0)


def sum_together(arrays, axis, dims):
    length = lax.axis_size(axis)
    blocks = [in_blocks(a, dim, length) for a, dim in zip(arrays, dims)]
    lines = jnp.concatenate([b.reshape(length, -1) for b in blocks], axis=1)
    width = max(16, -(-lines.shape[1] // 1024) * 8)
    lines = jnp.pad(lines, ((0, 0), (0, width * 128 - lines.shape[1]))).reshape(-1, 128)
    ravelled, at, outs = (lax.psum_scatter(lines, axis, tiled=True).reshape(-1), 0, [])
    for b in blocks:
        part = b[0]
        outs.append(ravelled[at : at + part.size].reshape(part.shape))
        at += part.size
    return tuple(outs)


def in_one(arrays, axis):
    ends = [0]
    for a in arrays:
        ends.append(ends[-1] + a.size)
    so_far = lax.psum(jnp.concatenate([a.ravel() for a in arrays]), axis)
    return tuple((so_far[b:e].reshape(a.shape) for a, b, e in zip(arrays, ends, ends[1:])))


def angles(positions, head_size):
    even_index = jnp.arange(0, head_size, 2).astype(jnp.float32)
    frequency = rope_base ** (-even_index / head_size)
    angle_grid = positions[:, None] * frequency[None, :]
    angle_grid = jnp.concatenate([angle_grid, angle_grid], axis=-1)
    return (jnp.cos(angle_grid), jnp.sin(angle_grid))


def rotate(values, cosine_table, sine_table):
    half_size = values.shape[-1] // 2
    turned = jnp.concatenate([-values[..., half_size:], values[..., :half_size]], axis=-1)
    return values * cosine_table + turned * sine_table


def norm_back(grad_normed, values, factor, gain):
    scaled = grad_normed * gain
    grad_gain = jnp.sum(grad_normed * values * factor, axis=0)
    grad_values = factor * (
        scaled - values * factor * factor * jnp.mean(scaled * values, axis=1, keepdims=True)
    )
    return (grad_values, grad_gain)


def per_device(
    tokens,
    cotangent,
    block_ids,
    routes,
    w_query,
    w_key,
    w_value,
    w_output,
    w_router,
    gain_attn,
    gain_moe,
    expert_gate,
    expert_up,
    expert_down,
):
    sequences, local_len, width = tokens.shape
    full_len = block_ids.shape[1]
    ep_size = lax.axis_size("ep")
    shard_index = lax.axis_index("ep")
    row_count = sequences * local_len
    top_count = routes.shape[2]
    local_experts = expert_gate.shape[0]
    all_experts = local_experts * ep_size
    capacity = 5 * row_count * top_count // (4 * all_experts)
    slot_total = all_experts * capacity
    group_size = HEADS // KV_HEADS
    kv_width = KV_HEADS * HD
    query_w, key_w, value_w, output_w, router_w, gain_a, gain_m = sent_together(
        (w_query, w_key, w_value, w_output, w_router, gain_attn, gain_moe), ("dp", "ep"), 0, 1
    )
    gain_a_f = gain_a.astype(jnp.float32)
    gain_m_f = gain_m.astype(jnp.float32)
    inputs = tokens.reshape(row_count, width).astype(jnp.float32)
    factor_a = lax.rsqrt(jnp.mean(inputs * inputs, axis=1, keepdims=True) + epsilon)
    normed = (inputs * factor_a * gain_a_f).astype(jnp.bfloat16)
    query_pre = jnp.dot(normed, query_w, preferred_element_type=jnp.float32)
    key_pre = jnp.dot(normed, key_w, preferred_element_type=jnp.float32)
    value_new = (
        jnp.dot(normed, value_w, preferred_element_type=jnp.float32)
        .astype(jnp.bfloat16)
        .reshape(sequences, local_len, kv_width)
    )
    positions = (shard_index * local_len + jnp.arange(local_len)).astype(jnp.float32)
    cosine_table, sine_table = angles(positions, HD)
    cosine_table = cosine_table[None, :, None, :]
    sine_table = sine_table[None, :, None, :]
    query_rot = rotate(
        query_pre.reshape(sequences, local_len, HEADS, HD), cosine_table, sine_table
    ).astype(jnp.bfloat16)
    key_rot = rotate(
        key_pre.reshape(sequences, local_len, KV_HEADS, HD), cosine_table, sine_table
    ).astype(jnp.bfloat16)
    key_rot = key_rot.reshape(sequences, local_len, kv_width)
    key_all, value_all = sent_together_2((key_rot, value_new), "ep", 1, 0)
    query_grp = query_rot.reshape(sequences, local_len, KV_HEADS, group_size, HD)
    key_heads = key_all.reshape(sequences, full_len, KV_HEADS, HD)
    value_heads = value_all.reshape(sequences, full_len, KV_HEADS, HD)
    own_blocks = lax.dynamic_slice_in_dim(block_ids, shard_index * local_len, local_len, 1)
    allowed = block_ids[:, None, None, None, :] <= own_blocks[:, None, None, :, None]
    raw_scores = (
        jnp.einsum("sqgrd,skgd->sgrqk", query_grp, key_heads, preferred_element_type=jnp.float32)
        * score_scale
    )
    scores = jnp.where(allowed, raw_scores, masked_value)
    row_peak = jnp.max(scores, axis=-1, keepdims=True)
    exponent = jnp.exp(scores - row_peak)
    row_sum = jnp.sum(exponent, axis=-1, keepdims=True)
    log_total = row_peak + jnp.log(row_sum)
    probabilities = (exponent / row_sum).astype(jnp.bfloat16)
    attended = jnp.einsum(
        "sgrqk,skgd->sqgrd", probabilities, value_heads, preferred_element_type=jnp.float32
    )
    attended = attended.reshape(row_count, width).astype(jnp.bfloat16)
    branch = jnp.dot(attended, output_w, preferred_element_type=jnp.float32)
    middle = inputs + residual_scale * branch
    factor_m = lax.rsqrt(jnp.mean(middle * middle, axis=1, keepdims=True) + epsilon)
    moe_in = (middle * factor_m * gain_m_f).astype(jnp.bfloat16)
    logits = jnp.dot(moe_in, router_w, preferred_element_type=jnp.float32)
    flat_routes = routes.reshape(row_count * top_count)
    one_hot = (flat_routes[:, None] == jnp.arange(all_experts)[None, :]).astype(jnp.int32)
    one_hot_f = one_hot.astype(jnp.float32).reshape(row_count, top_count, all_experts)
    chosen = jnp.sum(one_hot_f * logits[:, None, :], axis=-1)
    gate_weights = jax.nn.softmax(chosen, axis=-1)
    slot_index = jnp.sum((jnp.cumsum(one_hot, axis=0) - one_hot) * one_hot, axis=1)
    destination = jnp.where(slot_index < capacity, flat_routes * capacity + slot_index, slot_total)
    assignment = jnp.arange(row_count * top_count)
    source = (
        jnp.full((slot_total + 1,), row_count, jnp.int32)
        .at[destination]
        .set(assignment // top_count)[:slot_total]
    )
    assign_src = (
        jnp.full((slot_total + 1,), row_count * top_count, jnp.int32)
        .at[destination]
        .set(assignment)[:slot_total]
    )
    zero_row = jnp.zeros((1, width), jnp.bfloat16)
    outgoing = jnp.concatenate([moe_in, zero_row])[source].reshape(
        ep_size, local_experts, capacity, width
    )
    arrived = lax.all_to_all(outgoing, "ep", split_axis=0, concat_axis=0, tiled=True)
    gate_pre = jnp.einsum(
        "necd,edf->necf", arrived, expert_gate, preferred_element_type=jnp.float32
    )
    up_pre = jnp.einsum("necd,edf->necf", arrived, expert_up, preferred_element_type=jnp.float32)
    hidden = (jax.nn.silu(gate_pre) * up_pre).astype(jnp.bfloat16)
    result = jnp.einsum(
        "necf,efd->necd", hidden, expert_down, preferred_element_type=jnp.float32
    ).astype(jnp.bfloat16)
    returned, arrived = (result, arrived)
    coming = lax.all_to_all(returned, "ep", split_axis=0, concat_axis=0, tiled=True)
    expert_rows = jnp.concatenate([coming.reshape(slot_total, width), zero_row])
    picked = expert_rows[destination].reshape(row_count, top_count, width).astype(jnp.float32)
    mixture = jnp.sum(gate_weights[:, :, None] * picked, axis=1)
    output = (
        (middle + residual_scale * mixture)
        .astype(jnp.bfloat16)
        .reshape(sequences, local_len, width)
    )
    grad_y = cotangent.reshape(row_count, width).astype(jnp.float32)
    grad_mix = residual_scale * grad_y
    grad_pick = (gate_weights[:, :, None] * grad_mix[:, None, :]).astype(jnp.bfloat16)
    grad_gates = jnp.sum(picked * grad_mix[:, None, :], axis=-1)
    grad_rows = jnp.concatenate([grad_pick.reshape(row_count * top_count, width), zero_row])
    back_out = grad_rows[assign_src].reshape(ep_size, local_experts, capacity, width)
    grad_returned = lax.all_to_all(back_out, "ep", split_axis=0, concat_axis=0, tiled=True)
    gate_pre = jnp.einsum(
        "necd,edf->necf", arrived, expert_gate, preferred_element_type=jnp.float32
    )
    up_pre = jnp.einsum("necd,edf->necf", arrived, expert_up, preferred_element_type=jnp.float32)
    gate_sigmoid = jax.nn.sigmoid(gate_pre)
    silu_gate = gate_pre * gate_sigmoid
    hidden = (silu_gate * up_pre).astype(jnp.bfloat16)
    grad_hidden = jnp.einsum(
        "necd,efd->necf", grad_returned, expert_down, preferred_element_type=jnp.float32
    )
    grad_down_w = jnp.einsum(
        "necf,necd->efd", hidden, grad_returned, preferred_element_type=jnp.float32
    )
    grad_gate_pre = (
        grad_hidden * up_pre * gate_sigmoid * (1.0 + gate_pre * (1.0 - gate_sigmoid))
    ).astype(jnp.bfloat16)
    grad_up_pre = (grad_hidden * silu_gate).astype(jnp.bfloat16)
    grad_gate_w = jnp.einsum(
        "necd,necf->edf", arrived, grad_gate_pre, preferred_element_type=jnp.float32
    )
    grad_up_w = jnp.einsum(
        "necd,necf->edf", arrived, grad_up_pre, preferred_element_type=jnp.float32
    )
    grad_arrived = (
        jnp.einsum("necf,edf->necd", grad_gate_pre, expert_gate, preferred_element_type=jnp.float32)
        + jnp.einsum("necf,edf->necd", grad_up_pre, expert_up, preferred_element_type=jnp.float32)
    ).astype(jnp.bfloat16)
    grad_back = lax.all_to_all(grad_arrived, "ep", split_axis=0, concat_axis=0, tiled=True)
    grad_flat = jnp.concatenate([grad_back.reshape(slot_total, width), zero_row])
    grad_moe_in = jnp.sum(
        grad_flat[destination].reshape(row_count, top_count, width).astype(jnp.float32), axis=1
    )
    grad_chosen = gate_weights * (
        grad_gates - jnp.sum(gate_weights * grad_gates, axis=-1, keepdims=True)
    )
    grad_logits = jnp.sum(one_hot_f * grad_chosen[:, :, None], axis=1).astype(jnp.bfloat16)
    grad_router_w = jnp.einsum("rd,re->de", moe_in, grad_logits, preferred_element_type=jnp.float32)
    grad_moe_in = grad_moe_in + jnp.einsum(
        "re,de->rd", grad_logits, router_w, preferred_element_type=jnp.float32
    )
    grad_mid_norm, grad_gain_m = norm_back(grad_moe_in, middle, factor_m, gain_m_f)
    grad_middle = grad_y + grad_mid_norm
    grad_branch = (residual_scale * grad_middle).astype(jnp.bfloat16)
    grad_output_w = jnp.einsum(
        "rd,re->de", attended, grad_branch, preferred_element_type=jnp.float32
    )
    grad_attended = jnp.einsum(
        "re,de->rd", grad_branch, output_w, preferred_element_type=jnp.float32
    ).astype(jnp.bfloat16)
    grad_att_grp = grad_attended.reshape(sequences, local_len, KV_HEADS, group_size, HD)
    again_scores = jnp.where(
        allowed,
        jnp.einsum("sqgrd,skgd->sgrqk", query_grp, key_heads, preferred_element_type=jnp.float32)
        * score_scale,
        masked_value,
    )
    probs_full = jnp.exp(again_scores - log_total)
    grad_probs = jnp.einsum(
        "sqgrd,skgd->sgrqk", grad_att_grp, value_heads, preferred_element_type=jnp.float32
    )
    grad_scores = (
        probs_full * (grad_probs - jnp.sum(probs_full * grad_probs, axis=-1, keepdims=True))
    ).astype(jnp.bfloat16)
    grad_query_rot = score_scale * jnp.einsum(
        "sgrqk,skgd->sqgrd", grad_scores, key_heads, preferred_element_type=jnp.float32
    )
    grad_key_part = score_scale * jnp.einsum(
        "sgrqk,sqgrd->skgd", grad_scores, query_grp, preferred_element_type=jnp.float32
    )
    grad_value_part = jnp.einsum(
        "sgrqk,sqgrd->skgd", probabilities, grad_att_grp, preferred_element_type=jnp.float32
    )
    grad_key_sum, grad_value_sum = in_one_piece(
        (
            grad_key_part.reshape(sequences, full_len, kv_width),
            grad_value_part.reshape(sequences, full_len, kv_width),
        ),
        "ep",
        1,
        0,
    )
    grad_query_in = rotate(
        grad_query_rot.reshape(sequences, local_len, HEADS, HD), cosine_table, -sine_table
    )
    grad_query_in = grad_query_in.astype(jnp.bfloat16).reshape(row_count, width)
    grad_key_in = rotate(
        grad_key_sum.reshape(sequences, local_len, KV_HEADS, HD), cosine_table, -sine_table
    )
    grad_key_in = grad_key_in.astype(jnp.bfloat16).reshape(row_count, kv_width)
    grad_value_in = grad_value_sum.astype(jnp.bfloat16).reshape(row_count, kv_width)
    grad_query_w = jnp.einsum(
        "rd,re->de", normed, grad_query_in, preferred_element_type=jnp.float32
    )
    grad_key_w = jnp.einsum("rd,re->de", normed, grad_key_in, preferred_element_type=jnp.float32)
    grad_value_w = jnp.einsum(
        "rd,re->de", normed, grad_value_in, preferred_element_type=jnp.float32
    )
    grad_normed = (
        jnp.einsum("re,de->rd", grad_query_in, query_w, preferred_element_type=jnp.float32)
        + jnp.einsum("re,de->rd", grad_key_in, key_w, preferred_element_type=jnp.float32)
        + jnp.einsum("re,de->rd", grad_value_in, value_w, preferred_element_type=jnp.float32)
    )
    grad_in_norm, grad_gain_a = norm_back(grad_normed, inputs, factor_a, gain_a_f)
    grad_tokens = (
        (grad_middle + grad_in_norm).astype(jnp.bfloat16).reshape(sequences, local_len, width)
    )
    sum_query, sum_key, sum_value, sum_output, sum_router, sum_gain_a, sum_gain_m = sum_together(
        (
            grad_query_w,
            grad_key_w,
            grad_value_w,
            grad_output_w,
            grad_router_w,
            grad_gain_a,
            grad_gain_m,
        ),
        ("dp", "ep"),
        (0, 0, 0, 0, 0, 0, 0),
    )
    summed_gate, summed_up, summed_down = tuple(
        (
            part.astype(jnp.float32)
            for part in in_one(
                (
                    grad_gate_w.astype(jnp.bfloat16),
                    grad_up_w.astype(jnp.bfloat16),
                    grad_down_w.astype(jnp.bfloat16),
                ),
                "dp",
            )
        )
    )
    return (
        output,
        grad_tokens,
        sum_query,
        sum_key,
        sum_value,
        sum_output,
        sum_router,
        sum_gain_a,
        sum_gain_m,
        summed_gate,
        summed_up,
        summed_down,
    )


def solution(mesh):
    placed = (
        P("dp", "ep", None),
        P("dp", "ep", None),
        P("dp", None),
        P("dp", "ep", None),
        P(("dp", "ep"), None),
        P(("dp", "ep"), None),
        P(("dp", "ep"), None),
        P(("dp", "ep"), None),
        P(("dp", "ep"), None),
        P(("dp", "ep")),
        P(("dp", "ep")),
        P("ep", None, None),
        P("ep", None, None),
        P("ep", None, None),
    )
    return jax.shard_map(
        per_device,
        mesh=mesh,
        in_specs=placed,
        out_specs=(
            P("dp", "ep", None),
            P("dp", "ep", None),
            P(("dp", "ep"), None),
            P(("dp", "ep"), None),
            P(("dp", "ep"), None),
            P(("dp", "ep"), None),
            P(("dp", "ep"), None),
            P(("dp", "ep")),
            P(("dp", "ep")),
            P("ep", None, None),
            P("ep", None, None),
            P("ep", None, None),
        ),
        check_vma=False,
    )
```

profile of v0, /device:TPU:1, one launch (start us, length us, event | category | flops | bytes accessed | tf_op | source)
XLA Modules:
  0.0 975.5 jit_solution(4022226956694292944)
XLA Ops:
  12.4 71.5 %all-gather.3.cloned.1.call-done = bf16[1024,3106]{1,0:T(8,128)(2,1)} async-done(((bf16[8,3106]{1,0:T(8,128)(2,1)}), bf16[1024,3106]{1,0:T(8,128)(2,1)}) %all-gather.3.cloned.1.call-update) | async-done | bytes 6361104 | tf_op jit(solution)/shard_map/all_gather | solution.py:25
  92.4 9.1 reduce-window.6
  102.6 8.2 scatter_custom_fusion
  118.5 7.3 all-gather.5.cloned.1.call-done
  128.6 7.2 fusion.4
  135.8 9.4 fusion.3
  145.2 8.0 divide_convert_fusion
  161.0 8.8 gather_fusion
  174.9 8.1 scatter_custom_fusion.1
  188.1 14.8 %gather_fusion.2 = bf16[2560,1024]{1,0:T(8,128)(2,1)} fusion(bf16[2049,1024]{1,0:T(8,128)(2,1)} %concatenate.64, s32[3072]{0:T(1024)S(1)} %pad_clamp_fusion), kind=kCustom, calls=%fused_computation.2 | custom fusion | bytes 10496000 | tf_op jit(solution)/shard_map/gather | solution.py:222
  202.9 32.1 %all-to-all-done = bf16[8,4,80,1024]{3,2,1,0:T(8,128)(2,1)} async-done(((bf16[8,4,80,1024]{3,2,1,0:T(8,128)(2,1)}), bf16[8,4,80,1024]{3,2,1,0:T(8,128)(2,1)}, u32[]{:S(2)}, u32[]{:S(2)}) %all-to-all-start) | async-done | bytes 5242912 | tf_op jit(solution)/shard_map/all_to_all | solution.py:198
  240.5 9.1 fusion.22
  256.7 44.0 %all-to-all-done.2 = bf16[8,4,80,1024]{3,2,1,0:T(8,128)(2,1)} async-done(((bf16[8,4,80,1024]{3,2,1,0:T(8,128)(2,1)}), bf16[8,4,80,1024]{3,2,1,0:T(8,128)(2,1)}, u32[]{:S(2)}, u32[]{:S(2)}) %all-to-all-start.2) | async-done | bytes 5242912 | tf_op jit(solution)/shard_map/all_to_all | solution.py:223
  300.6 11.1 %fusion.11 = (bf16[8,4,80,512]{3,2,0,1:T(8,128)(2,1)}, bf16[8,4,80,512]{3,2,0,1:T(8,128)(2,1)}, bf16[8,4,80,512]{3,2,0,1:T(8,128)(2,1)S(1)}) fusion(f32[4,8,80,512]{3,2,1,0:T(8,128)} %fusion.22, f32[4,8,80,512]{3,2,1,0:T(8,128)} %fusion.24, bf16[4,512,1024]{2,1,0:T(8,128)(2,1)} %param.27, bf16[8,4,80,1024]{3,2,1,0:T(8,128)(2,1)} %all-to-all-done.2), kind=kOutput, calls=%fused_computation.35 | convolution fusion | flops 2704015360 | bytes 27787264 | tf_op jit(solution)/shard_map/necd,efd->necf/dot_general | solution.py:231
  317.4 8.4 fusion.8
  346.5 51.1 %all-to-all-done.3 = bf16[8,4,80,1024]{3,2,1,0:T(8,128)(2,1)} async-done(((bf16[8,4,80,1024]{3,2,1,0:T(8,128)(2,1)}), bf16[8,4,80,1024]{3,2,1,0:T(8,128)(2,1)}, u32[]{:S(2)}, u32[]{:S(2)}) %all-to-all-start.3) | async-done | bytes 5242912 | tf_op jit(solution)/shard_map/all_to_all | solution.py:251
  440.8 14.5 %gather_fusion.3 = bf16[2048,1024]{1,0:T(8,128)(2,1)} fusion(bf16[2561,1024]{1,0:T(8,128)(2,1)} %concatenate.65, s32[2048]{0:T(1024)S(1)} %broadcast_clamp_fusion), kind=kCustom, calls=%fused_computation.3 | custom fusion | bytes 8396800 | tf_op jit(solution)/shard_map/gather | solution.py:254
  468.6 14.2 %gather_fusion.1 = bf16[2048,1024]{1,0:T(8,128)(2,1)} fusion(bf16[2561,1024]{1,0:T(8,128)(2,1)} %concatenate.63, s32[2048]{0:T(1024)S(1)} %broadcast_clamp_fusion), kind=kCustom, calls=%fused_computation.1 | custom fusion | bytes 8396800 | tf_op jit(solution)/shard_map/gather | solution.py:210
  497.2 8.2 fusion.128
  505.4 11.7 %fusion = (f32[2,8,2,128]{3,2,1,0:T(2,128)S(1)}, f32[2,8,1024,128,2]{3,2,4,1,0:T(8,128)}) fusion(f32[2,8,1024,128,2]{3,2,4,1,0:T(8,128)} %get-tuple-element.55, f32[2,8,2,128]{3,2,1,0:T(2,128)S(1)} %bitcast.374, pred[2,128,1024]{1,2,0:T(8,128)(4,1)S(1)} %copy-done.11, bf16[2,1024,8,64,1]{1,3,4,2,0:T(8,128)(2,1)S(1)} %bitcast.335, ...), kind=kOutput, calls=%fused_computation.8 | convolution fusion | flops 557838336 | bytes 36470784 | tf_op jit(solution)/shard_map/sqgrd,skgd->sgrqk/dot_general | solution.py:281
  522.5 12.1 %fusion.2 = bf16[2,8,2,128,1024]{3,4,2,1,0:T(8,128)(2,1)S(1)} fusion(f32[2,8,1024,128,2]{3,2,4,1,0:T(8,128)} %get-tuple-element.60, f32[2,8,1024,128,2]{3,2,4,1,0:T(8,128)} %get-tuple-element.55, f32[2,8,2,128]{3,2,1,0:T(2,128)S(1)} %get-tuple-element.59, f32[2,8,2,128]{3,2,1,0:T(2,128)S(1)} %bitcast.375, pred[2,128,1024]{1,2,0:T(8,128)(4,1)S(1)} %copy-done.11), kind=kLoop, calls=%fused_computation.10 | loop fusion | flops 25165824 | bytes 42237952 | tf_op jit(solution)/shard_map/convert_element_type | solution.py:286
  544.7 7.8 pad_maximum_fusion.1
  552.6 15.7 %pad_maximum_fusion = bf16[6291456]{0:T(1024)(128)(2,1)} fusion(bf16[2097152]{0:T(1024)(128)(2,1)} %bitcast.341, bf16[2097152]{0:T(1024)(128)(2,1)} %bitcast.342, bf16[2097152]{0:T(1024)(128)(2,1)} %bitcast.343), kind=kLoop, calls=%fused_computation.16 | loop fusion | flops 37748736 | bytes 25165824 | tf_op jit(solution)/shard_map/concatenate | solution.py:70
  631.5 15.4 %concatenate.71 = f32[128,24848]{1,0:T(8,128)} concatenate(f32[128,8192]{1,0:T(8,128)} %reshape_reshape.15, f32[128,4096]{1,0:T(8,128)} %reshape_reshape.16, f32[128,4096]{1,0:T(8,128)} %reshape_reshape.17, f32[128,8192]{1,0:T(8,128)} %reshape_reshape.18, f32[128,256]{1,0:T(8,128)S(1)} %copy-done.34, f32[128,8]{1,0:T(8,128)S(1)} %reshape.600, f32[128,8]{1,0:T(8,128)S(1)} %reshape.601), dimensions={1} | concatenate | bytes 25444352 | tf_op jit(solution)/shard_map/concatenate | solution.py:55
  646.9 11.0 %pad.8 = f32[128,25600]{1,0:T(8,128)} pad(f32[128,24848]{1,0:T(8,128)} %concatenate.71, f32[]{:T(128)} %constant.26.clone.1), padding=0_0x0_752 | pad | bytes 25829380 | tf_op jit(solution)/shard_map/jit(_pad)/pad | solution.py:57
  657.9 12.3 %reshape.602 = f32[25600,128]{1,0:T(8,128)} reshape(f32[128,25600]{1,0:T(8,128)} %pad.8) | data formatting | bytes 26214400 | tf_op jit(solution)/shard_map/reshape | solution.py:57
  670.3 116.1 %all-reduce.9.cloned.1.call-done = bf16[6291456]{0:T(1024)(128)(2,1)} async-done(((bf16[6291456]{0:T(1024)(128)(2,1)}), bf16[6291456]{0:T(1024)(128)(2,1)}) %all-reduce.9.cloned.1.call-update) | async-done | bytes 12582928 | tf_op jit(solution)/shard_map/psum | solution.py:70
  786.3 11.6 %slice_convert_fusion = (f32[2097152]{0:T(1024)}, f32[2097152]{0:T(1024)}, f32[2097152]{0:T(1024)}) fusion(bf16[6291456]{0:T(1024)(128)(2,1)} %all-reduce.9.cloned.1.call-done), kind=kLoop, calls=%fused_computation.55 | loop fusion | flops 6291456 | bytes 37748736 | tf_op jit(solution)/shard_map/convert_element_type | solution.py:345
  797.9 9.3 reshape.618
  807.2 9.5 reshape.619
  816.7 9.4 reshape.620
  827.2 134.6 %all-reduce.11.cloned.1.call-done = f32[25600,128]{1,0:T(8,128)} async-done(((f32[25600,128]{1,0:T(8,128)}), f32[25600,128]{1,0:T(8,128)}) %all-reduce.11.cloned.1.call-update) | async-done | bytes 13107216
  (243 shorter events, 238.9 us)
Async XLA Ops:
  7.2 83.1 %copy-start.8 = (bf16[2,128,1024]{2,1,0:T(8,128)(2,1)S(1)}, bf16[2,128,1024]{2,1,0:T(8,128)(2,1)}, u32[]{:S(2)}) copy-start(bf16[2,128,1024]{2,1,0:T(8,128)(2,1)} %param.14) | copy-start | bytes 1572868
  7.2 76.7 %all-gather.3.cloned.1.call-start = ((), (), s32[]{:S(2)}) async-start(), calls=%async_computation.5 | async-start | bytes 6604800 | tf_op jit(solution)/shard_map/all_gather | solution.py:25
  10.3 115.6 %all-gather.5.cloned.1.call-start = ((), (), s32[]{:S(2)}) async-start(), calls=%async_computation.6 | async-start | bytes 4718592 | tf_op jit(solution)/shard_map/all_gather | solution.py:36
  11.1 107.1 %copy-start.31 = (f32[128,64]{0,1:T(8,128)}, f32[128,64]{0,1:T(8,128)S(1)}, u32[]{:S(2)}) copy-start(f32[128,64]{0,1:T(8,128)S(1)} %get-tuple-element.51) | copy-start | bytes 98308
  12.4 78.6 %copy-start.39 = (f32[256]{0:T(256)}, f32[256]{0:T(256)S(1)}, u32[]{:S(2)}) copy-start(f32[256]{0:T(256)S(1)} %get-tuple-element.53) | copy-start | bytes 3076
  90.5 26.9 %copy-start.6 = (bf16[2,128,1024]{2,1,0:T(8,128)(2,1)}, bf16[2,128,1024]{2,1,0:T(8,128)(2,1)S(1)}, u32[]{:S(2)}) copy-start(bf16[2,128,1024]{2,1,0:T(8,128)(2,1)S(1)} %fusion.72) | copy-start | bytes 1572868
  90.5 20.4 %copy-start.41 = (s32[2,1024]{1,0:T(2,128)S(1)}, s32[2,1024]{1,0:T(2,128)}, u32[]{:S(2)}) copy-start(s32[2,1024]{1,0:T(2,128)} %param.16) | copy-start | bytes 24580
  111.2 33.9 %copy-start.10 = (pred[2,128,1024]{1,2,0:T(8,128)(4,1)}, pred[2,128,1024]{1,2,0:T(8,128)(4,1)S(1)}, u32[]{:S(2)}) copy-start(pred[2,128,1024]{1,2,0:T(8,128)(4,1)S(1)} %broadcast_compare_fusion) | copy-start | bytes 786436
  118.5 17.3 %copy-start.18 = (bf16[2,128,16,64]{1,3,2,0:T(8,128)(2,1)}, bf16[2,128,16,64]{1,3,2,0:T(8,128)(2,1)S(1)}, u32[]{:S(2)}) copy-start(bf16[2,128,16,64]{1,3,2,0:T(8,128)(2,1)S(1)} %fusion.61) | copy-start | bytes 1572868
  128.5 7.3 copy-start.2
  128.6 24.6 %copy-start.4 = (bf16[2,1024,512]{1,2,0:T(8,128)(2,1)}, bf16[2,1024,512]{1,2,0:T(8,128)(2,1)S(1)}, u32[]{:S(2)}) copy-start(bf16[2,1024,512]{1,2,0:T(8,128)(2,1)S(1)} %get-tuple-element.31) | copy-start | bytes 6291460
  160.9 22.2 %copy-start.16 = (bf16[256,1024]{1,0:T(8,128)(2,1)}, bf16[256,1024]{1,0:T(8,128)(2,1)S(1)}, u32[]{:S(2)}) copy-start(bf16[256,1024]{1,0:T(8,128)(2,1)S(1)} %multiply_convert_fusion.1) | copy-start | bytes 1572868
  169.8 13.2 %copy-start.28 = (bf16[2,128,1024]{2,1,0:T(8,128)(2,1)S(1)}, bf16[2,128,1024]{2,1,0:T(8,128)(2,1)}, u32[]{:S(2)}) copy-start(bf16[2,128,1024]{2,1,0:T(8,128)(2,1)} %param.15) | copy-start | bytes 1572868
  169.8 65.3 %all-to-all-start = ((bf16[8,4,80,1024]{3,2,1,0:T(8,128)(2,1)}), bf16[8,4,80,1024]{3,2,1,0:T(8,128)(2,1)}, u32[]{:S(2)}, u32[]{:S(2)}) async-start(bf16[8,4,80,1024]{3,2,1,0:T(8,128)(2,1)} %bitcast.336), calls=%async_computation | async-start | bytes 10485760 | tf_op jit(solution)/shard_map/all_to_all | solution.py:198
  235.1 65.6 %all-to-all-start.2 = ((bf16[8,4,80,1024]{3,2,1,0:T(8,128)(2,1)}), bf16[8,4,80,1024]{3,2,1,0:T(8,128)(2,1)}, u32[]{:S(2)}, u32[]{:S(2)}) async-start(bf16[8,4,80,1024]{3,2,1,0:T(8,128)(2,1)} %bitcast.337), calls=%async_computation.2 | async-start | bytes 10485760 | tf_op jit(solution)/shard_map/all_to_all | solution.py:223
  240.5 9.1 copy-start.21
  331.6 66.0 %all-to-all-start.3 = ((bf16[8,4,80,1024]{3,2,1,0:T(8,128)(2,1)}), bf16[8,4,80,1024]{3,2,1,0:T(8,128)(2,1)}, u32[]{:S(2)}, u32[]{:S(2)}) async-start(bf16[8,4,80,1024]{3,2,1,0:T(8,128)(2,1)} %copy.197), calls=%async_computation.3 | async-start | bytes 10485760 | tf_op jit(solution)/shard_map/all_to_all | solution.py:251
  397.6 65.6 %all-to-all-start.1 = ((bf16[8,4,80,1024]{3,2,1,0:T(8,128)(2,1)}), bf16[8,4,80,1024]{3,2,1,0:T(8,128)(2,1)}, u32[]{:S(2)}, u32[]{:S(2)}) async-start(bf16[8,4,80,1024]{3,2,1,0:T(8,128)(2,1)} %copy.194), calls=%async_computation.1 | async-start | bytes 10485760 | tf_op jit(solution)/shard_map/all_to_all | solution.py:208
  403.0 204.3 %reduce-scatter.2.cloned.1.call-start = ((), (), s32[]{:S(2)}) async-start(), calls=%async_computation.7 | async-start | bytes 9437184 | tf_op jit(solution)/shard_map/reduce_scatter | solution.py:42
  468.6 14.2 %copy-start.13 = (f32[256,1024]{1,0:T(8,128)S(1)}, f32[256,1024]{1,0:T(8,128)}, u32[]{:S(2)}) copy-start(f32[256,1024]{1,0:T(8,128)} %copy-done.12) | copy-start | bytes 3145732
  482.8 6.3 copy-start.15
  497.2 8.2 copy-start.5
  497.2 8.2 copy-start.11
  522.5 12.1 %copy-start.19 = (bf16[2,128,16,64]{1,3,2,0:T(8,128)(2,1)S(1)}, bf16[2,128,16,64]{1,3,2,0:T(8,128)(2,1)}, u32[]{:S(2)}) copy-start(bf16[2,128,16,64]{1,3,2,0:T(8,128)(2,1)} %copy-done.18) | copy-start | bytes 1572868
  552.6 233.8 %all-reduce.9.cloned.1.call-start = ((), (), s32[]{:S(2)}) async-start(), calls=%async_computation.8 | async-start | bytes 25165824 | tf_op jit(solution)/shard_map/psum | solution.py:70
  568.4 393.4 %all-reduce.11.cloned.1.call-start = ((), (), s32[]{:S(2)}) async-start(), calls=%async_computation.9 | async-start | bytes 26214400
  594.9 8.6 copy-start.20
  607.3 7.6 copy-start.23
  620.5 7.1 copy-start.22
  620.5 7.1 copy-start.27
  623.4 6.0 copy-start.38
  623.4 6.0 copy-start.40
  (19 other events, 75.4 us)
Sparse Core Ops, SparseCore 0:
  11.6 72.2 all-gather.2
  92.1 33.6 all-gather.4
  552.7 51.4 reduce-scatter.1
  607.6 178.7 all-reduce.8
  792.1 169.6 all-reduce.10
where the time goes:
time: 983 us; the launch traced here: 976 us
  waiting for transfers between devices  459 us (47%)
  local copies, waits for them, and re-layouts  240 us (24%)
  matrix products  137 us (14%)
  other arithmetic  102 us (10%)
  starting transfers between devices  22 us (2%)
  between operations  15 us (2%)
    unnamed x6, waiting for transfers between devices  135 us
    psum x1, waiting for transfers between devices, in_one(): so_far = lax.psum(jnp.concatenate([a.ravel() for a in arrays]), axis)  116 us
    all_gather x1, waiting for transfers between devices, sent_together(): out = lax.all_gather(both, axis, axis=dim, tiled=True)  71.5 us
    all_to_all x1, waiting for transfers between devices, per_device(): lax.all_to_all(grad_arrived, 'ep', split_axis=0, concat_axis=0, tiled=True)  51.1 us
    all_to_all x1, waiting for transfers between devices, per_device(): lax.all_to_all(back_out, 'ep', split_axis=0, concat_axis=0, tiled=True)  44 us
    all_to_all x1, waiting for transfers between devices, per_device(): lax.all_to_all(outgoing, 'ep', split_axis=0, concat_axis=0, tiled=True)  32.1 us
    convert_element_type x3, local copies, waits for them, and re-layouts, per_device(): part.astype(jnp.float32)  28.2 us
  transfers between devices with their start and end apart: 9, of which 8 were waited for; matrix products, arithmetic and copies ran while one was open for 30% of the time, Pallas kernels for 0%

commit v1 on v0

v1 whole, which is shorter than its diff:
```python
import math

import jax
import jax.numpy as jnp
import numpy as np
from jax import lax
from jax.experimental import pallas as pl
from jax.experimental.pallas import tpu as pltpu
from jax.sharding import PartitionSpec as P

MESH = pl.DeviceIdType.MESH
BF = jnp.bfloat16
F32 = jnp.float32
ANY = pl.BlockSpec(memory_space=pl.ANY)
VM = pl.BlockSpec(memory_space=pltpu.VMEM)

DP, EP, CHIPS = 16, 8, 4
D, HD, F = 1024, 64, 512
ROWS, HALF, LEN, SEQS = 256, 128, 1024, 2
EXPERTS, OWN, CAP = 32, 4, 80
SLOTS = EP * CAP
EPS = 1e-6
RES = 0.22
SCORE = 0.015625
LOG2E = 1.4426950408889634
MASKED = -1e30
MIB = 2**20


def nt(a, b):
    return lax.dot_general(a, b, (((1,), (1,)), ((), ())), preferred_element_type=F32)


def nn(a, b):
    return jnp.dot(a, b, preferred_element_type=F32)


def tn(a, b):
    return lax.dot_general(a, b, (((0,), (0,)), ((), ())), preferred_element_type=F32)


def place():
    e = lax.axis_index("ep")
    return lax.axis_index("dp"), e, e // 2, lax.rem(e, 2)


def greet(peers):
    b = pltpu.get_barrier_semaphore()
    for p in peers:
        pl.semaphore_signal(b, inc=1, device_id=p, device_id_type=MESH)
    return lambda: pl.semaphore_wait(b, len(peers))


def ep_peers(d, e):
    return [(d, lax.rem(e + k, EP)) for k in range(1, EP)]


def dp_peers(d, e):
    return [(lax.rem(d + k, DP), e) for k in range(1, DP)]


class Sender:
    def __init__(self, ss, rs):
        self.ss, self.rs, self.n = ss, rs, 0

    def __call__(self, src, dst, dev):
        i = self.n
        self.n += 1
        cp = pltpu.make_async_remote_copy(
            src, dst, self.ss.at[i], self.rs.at[i], device_id=dev, device_id_type=MESH
        )
        cp.start()
        return cp


def ring(out, d, e, z, c, send):
    right, left = (d, lax.rem(z + 1, CHIPS) * 2 + c), (d, lax.rem(z + 3, CHIPS) * 2 + c)
    part = (d, z * 2 + 1 - c)
    er, el, eo = right[1], left[1], lax.rem(z + 2, CHIPS) * 2 + c

    def start(src0, src1, half):
        if half == 0:
            return [
                send(src0, out.at[e, 0], right),
                send(src0, out.at[e, 0], left),
                send(src0, out.at[e, 0], part),
            ]
        return [
            send(src1, out.at[e, 1], left),
            send(src1, out.at[e, 1], right),
            send(src1, out.at[e, 1], part),
        ]

    def finish(a, b):
        (r0, l0, p0), (l1, r1, p1) = a, b
        f = []
        r0.wait_recv()
        fr = send(out.at[el, 0], out.at[el, 0], right)
        f.append(send(out.at[el, 0], out.at[el, 0], part))
        l1.wait_recv()
        fl = send(out.at[er, 1], out.at[er, 1], left)
        f.append(send(out.at[er, 1], out.at[er, 1], part))
        r1.wait_recv()
        f.append(send(out.at[el, 1], out.at[el, 1], part))
        l0.wait_recv()
        f.append(send(out.at[er, 0], out.at[er, 0], part))
        fr.wait_recv()
        f.append(send(out.at[eo, 0], out.at[eo, 0], part))
        fl.wait_recv()
        f.append(send(out.at[eo, 1], out.at[eo, 1], part))
        for cp in (r0, l0, l1, r1, fr, fl):
            cp.wait_send()
        for cp in [p0, p1] + f:
            cp.wait()

    return start, finish


def remote_call(body, cid, outs, ins, specs, scratch, sems, out_specs=None, vmem=48, flops=0):
    return pl.pallas_call(
        body,
        name=body.__name__,
        out_shape=outs,
        in_specs=specs,
        out_specs=out_specs if out_specs is not None else [ANY] * len(outs),
        scratch_shapes=[
            *scratch,
            pltpu.SemaphoreType.DMA((4,)),
            pltpu.SemaphoreType.DMA((sems,)),
            pltpu.SemaphoreType.DMA((sems,)),
        ],
        compiler_params=pltpu.CompilerParams(
            collective_id=cid, has_side_effects=True, vmem_limit_bytes=vmem * MIB
        ),
        cost_estimate=pl.CostEstimate(flops=flops, bytes_accessed=20 * MIB, transcendentals=0),
    )(*ins)


def sds(shape, dtype):
    return jax.ShapeDtypeStruct(shape, dtype)


def gather_inputs(x, rt, wq, wk, wv, wo, sm, xall, rall, wsl, wof, wp, wop, ls, ss, rs):
    d, e, z, c = place()
    wait = greet(ep_peers(d, e) + dp_peers(d, e))
    q, k, v = wq[...].astype(F32), wk[...].astype(F32), wv[...].astype(F32)
    small = sm[...].astype(F32)
    for t in range(EP):
        row = jnp.concatenate(
            [
                q[:, 128 * t : 128 * t + 128],
                k[:, 64 * t : 64 * t + 64],
                v[:, 64 * t : 64 * t + 64],
            ],
            axis=1,
        )
        wp[t] = jnp.concatenate([row, small], axis=0).astype(BF)
    o = wo[...].astype(F32)
    wop[...] = jnp.concatenate([o[:, :512], o[:, 512:]], axis=0).astype(BF)
    wait()
    send = Sender(ss, rs)
    own = [
        pltpu.make_async_copy(x, xall.at[e], ls.at[0]),
        pltpu.make_async_copy(wp.at[e], wsl.at[d, e], ls.at[1]),
        pltpu.make_async_copy(wop, wof.at[d, e], ls.at[2]),
        pltpu.make_async_copy(rt, rall.at[e], ls.at[3]),
    ]
    for cp in own:
        cp.start()
    first = []
    for k in range(1, EP):
        t = lax.rem(e + k, EP)
        first.append(send(wp.at[t], wsl.at[d, e], (d, t)))
    for k in range(1, EP):
        t = lax.rem(e + k, EP)
        first.append(send(wop, wof.at[d, e], (d, t)))
    start, finish = ring(xall, d, e, z, c, send)
    a = start(x.at[0], x.at[1], 0)
    b = start(x.at[0], x.at[1], 1)
    routes = [send(rt, rall.at[e], p) for p in ep_peers(d, e)]
    own[1].wait()
    for cp in first[: EP - 1]:
        cp.wait_recv()
    second = [send(wsl.at[d], wsl.at[d], p) for p in dp_peers(d, e)]
    own[2].wait()
    for cp in first[EP - 1 :]:
        cp.wait_recv()
    mine = pl.ds(c * 4, 4)
    third = [send(wof.at[d, mine], wof.at[d, mine], p) for p in dp_peers(d, e)]
    finish(a, b)
    part = (d, z * 2 + 1 - c)
    last = []
    for k, cp in enumerate(third):
        cp.wait_recv()
        s = lax.rem(d + DP - 1 - k, DP)
        last.append(send(wof.at[s, mine], wof.at[s, mine], part))
    for cp in first + third:
        cp.wait_send()
    for cp in routes + second + last:
        cp.wait()
    own[0].wait()
    own[3].wait()


def lanes(shape):
    return lax.broadcasted_iota(jnp.int32, shape, 1)


def turn(v):
    first = lax.rem(lanes(v.shape), HD) < HD // 2
    return jnp.where(first, -pltpu.roll(v, 128 - HD // 2, 1), pltpu.roll(v, HD // 2, 1))


def both(kv):
    low = lanes(kv.shape) < HD
    other = pltpu.roll(kv, HD, 1)
    return jnp.where(low, kv, other).astype(BF), jnp.where(low, other, kv).astype(BF)


def two_heads(v):
    low = lanes(v.shape) < HD
    zero = jnp.zeros_like(v)
    return jnp.concatenate([jnp.where(low, v, zero), jnp.where(low, zero, v)], axis=0)


def spans(i):
    return i * ROWS, min(LEN, i * ROWS + 2 * ROWS)


def project_attend(
    x, wsl, wof, cs, sn, ids, q_o, kv_o, nrm_o, att_o, lse_o, gt_o, wo_o, w_s, kk_s, vv_s
):
    @pl.when(pl.program_id(0) == 0)
    def _():
        w = wsl[...].astype(F32).reshape(D // 8, 16, 256)
        w_s[...] = w[:, :8].reshape(D, 256).astype(BF)
        gt_o[...] = w[:, 8:].reshape(D, 256)[:, :128].T
        for i in range(4):
            o = wof[4 * i : 4 * i + 4].astype(F32).reshape(32, 16, 512)
            wo_o[256 * i : 256 * i + 256, :512] = o[:, :8].reshape(256, 512).astype(BF)
            wo_o[256 * i : 256 * i + 256, 512:] = o[:, 8:].reshape(256, 512).astype(BF)

    gain = gt_o[32:33, :]
    for r in range(4):
        rows = slice(256 * r, 256 * r + 256)
        v = x[2 * r : 2 * r + 2, 0].astype(F32).reshape(256, D)
        factor = lax.rsqrt(jnp.mean(v * v, axis=1, keepdims=True) + EPS)
        n = (v * factor * gain).astype(BF)
        nrm_o[0, rows] = n
        pre = nn(n, w_s[...])
        co, si = cs[rows], sn[rows]
        q, kv = pre[:, :128], pre[:, 128:]
        q_o[0, rows] = (q * co + turn(q) * si).astype(BF)
        kv = jnp.where(lanes(kv.shape) < HD, kv * co + turn(kv) * si, kv).astype(BF)
        kv_o[0, rows] = kv
        kk_s[rows], vv_s[rows] = both(kv.astype(F32))
    ids_k = ids[0]
    ids_q = jnp.broadcast_to(ids_k, (128, LEN)).T[:, :1]
    for i in range(4):
        q2 = two_heads(q_o[0, ROWS * i : ROWS * i + ROWS].astype(F32)).astype(BF)
        own = ids_q[ROWS * i : ROWS * i + ROWS]
        own = jnp.concatenate([own, own], axis=0)
        at, end = spans(i)
        parts = []
        if at:
            parts.append((nt(q2, kk_s[:at]) * (SCORE * LOG2E), slice(0, at)))
        t = nt(q2, kk_s[at:end]) * (SCORE * LOG2E)
        parts.append((jnp.where(ids_k[:, at:end] <= own, t, MASKED), slice(at, end)))
        peak = parts[0][0].max(axis=1, keepdims=True)
        for t, _ in parts[1:]:
            peak = jnp.maximum(peak, t.max(axis=1, keepdims=True))
        total, out = 0.0, 0.0
        for t, span in parts:
            p = jnp.exp2(t - peak)
            total = total + p.sum(axis=1, keepdims=True)
            out = out + nn(p.astype(BF), vv_s[span])
        out = out * (1.0 / total)
        lse = jnp.broadcast_to(peak + jnp.log2(total), (2 * ROWS, 128))
        low = lanes((ROWS, 128)) < HD
        att = jnp.where(low, out[:ROWS], out[ROWS:]).astype(BF)
        att_o[2 * i : 2 * i + 2, 0] = att.reshape(2, HALF, 128)
        lse_o[0, ROWS * i : ROWS * i + ROWS] = jnp.where(low, lse[:ROWS], lse[ROWS:])


def attended_to_moe(att, x, wo, gt, moe, mid_o, own_o, at_o, arr, mo, ls, ss, rs):
    d, e, z, c = place()
    greet(ep_peers(d, e))()
    send = Sender(ss, rs)
    lc = pltpu.make_async_copy(att.at[e], arr.at[e], ls.at[0])
    lc.start()
    cps = []
    for k in (4, 3, 5, 2, 6, 1, 7):
        t = lax.rem(e + k, EP)
        cps.append(send(att.at[t], arr.at[e], (d, t)))
    lc.wait()
    for cp in cps:
        cp.wait_recv()
    start, finish = ring(moe, d, e, z, c, send)
    gain = gt[33:34, :]
    begun, own = [], []
    for h in range(2):
        rows = slice(HALF * h, HALF * h + HALF)
        a = jnp.concatenate([arr[s, rows] for s in range(EP)], axis=1)
        at_o[rows] = a
        m = x[rows].astype(F32) + RES * nn(a, wo[...])
        mid_o[rows] = m
        factor = lax.rsqrt(jnp.mean(m * m, axis=1, keepdims=True) + EPS)
        n = (m * factor * gain).astype(BF)
        mo[h] = n
        own_o[rows] = n
        own.append(pltpu.make_async_copy(mo.at[h], moe.at[e, h], ls.at[1 + h]))
        own[h].start()
        begun.append(start(mo.at[0], mo.at[1], h))
    finish(*begun)
    for cp in cps:
        cp.wait_send()
    for cp in own:
        cp.wait()


def routing(rt, logits_t):
    ids = lax.broadcasted_iota(jnp.int32, (EXPERTS, ROWS), 0)
    hit = rt[0:1] == ids
    for k in range(1, 8):
        hit = hit | (rt[k : k + 1] == ids)
    w = jnp.where(hit, logits_t, MASKED)
    w = jnp.where(hit, jnp.exp(w - w.max(axis=0, keepdims=True)), 0.0)
    gates = w / w.sum(axis=0, keepdims=True)
    earlier = lax.broadcasted_iota(jnp.int32, (ROWS, ROWS), 0) < lax.broadcasted_iota(
        jnp.int32, (ROWS, ROWS), 1
    )
    slot = nn(jnp.where(hit, 1.0, 0.0).astype(BF), jnp.where(earlier, 1.0, 0.0).astype(BF))
    return gates, jnp.where(hit, slot, -1.0)


def experts_weights(moe, cot, rall, gt, wg, wu, wd, dw_o, hs_o, dg_o, du_o, gg_o, p_o, x_s, y_s, g_s):
    j = pl.program_id(0)
    first = lax.axis_index("ep") * OWN

    @pl.when(j == 0)
    def _():
        router_t = gt[:EXPERTS].astype(BF)
        row = lax.broadcasted_iota(jnp.int32, (EXPERTS, ROWS), 0)
        place_in = lax.broadcasted_iota(jnp.int32, (CAP, ROWS), 0).astype(F32)

        def source(s, carry):
            m = moe[s]
            gates, slot = routing(rall[s], nt(router_t, m))
            picks = []
            for i in range(OWN):
                sel = row == first + i
                pick = jnp.sum(jnp.where(sel, slot, 0.0), axis=0, keepdims=True) == place_in
                gate = jnp.sum(jnp.where(sel, gates, 0.0), axis=0, keepdims=True)
                g = jnp.sum(jnp.where(pick, gate, 0.0), axis=1, keepdims=True)
                g_s[i, pl.ds(pl.multiple_of(s * CAP, 16), CAP)] = jnp.broadcast_to(g, (CAP, 128))
                picks.append(jnp.where(pick, 1.0, 0.0).astype(BF))
            pick = jnp.concatenate(picks, axis=0)
            p_o[s] = pick
            xs = nn(pick, m).astype(BF)
            ys = nn(pick, cot[s]).astype(BF)
            for i in range(OWN):
                at = pl.ds(pl.multiple_of(s * CAP, 16), CAP)
                x_s[i, at] = xs[CAP * i : CAP * i + CAP]
                y_s[i, at] = ys[CAP * i : CAP * i + CAP]
            return carry

        lax.fori_loop(0, EP, source, 0)

    x, y = x_s[j], y_s[j]
    gate = g_s[j][:, :1] * RES
    g = nn(x, wg[0])
    u = nn(x, wu[0])
    dh = nt(y, wd[0])
    s = 1.0 / (1.0 + jnp.exp(-g))
    silu = g * s
    h = silu * u
    gg_o[0] = jnp.broadcast_to(RES * jnp.sum(h * dh, axis=1, keepdims=True), (SLOTS, 128))
    dh = dh * gate
    hs = (h * gate).astype(BF)
    dg = (dh * u * s * (1.0 + g * (1.0 - s))).astype(BF)
    du = (dh * silu).astype(BF)
    hs_o[0], dg_o[0], du_o[0] = hs, dg, du
    w = tn(x, jnp.concatenate([dg, du], axis=1))
    dw_o[0, :D] = w[:, :F].astype(BF)
    dw_o[0, D : 2 * D] = w[:, F:].astype(BF)
    w = tn(hs, y)
    dw_o[0, 2 * D : 2 * D + F] = w[:, :F].astype(BF)
    dw_o[0, 2 * D + F :] = w[:, F:].astype(BF)


def experts_back(hs, dg, du, gg, picks, wg, wu, wd, part_o, gg_o, eo_s, dx_s):
    j = pl.program_id(0)
    eo = nn(hs[0], wd[0]).astype(BF)
    dx = (nt(dg[0], wg[0]) + nt(du[0], wu[0])).astype(BF)
    for s in range(EP):
        eo_s[s, pl.ds(pl.multiple_of(j * CAP, 16), CAP)] = eo[CAP * s : CAP * s + CAP]
        dx_s[s, pl.ds(pl.multiple_of(j * CAP, 16), CAP)] = dx[CAP * s : CAP * s + CAP]

    @pl.when(j == OWN - 1)
    def _():
        def back(s, carry):
            p = picks[s]
            part_o[s, :, :D] = tn(p, eo_s[s]).astype(BF)
            part_o[s, :, D:] = tn(p, dx_s[s]).astype(BF)
            at = pl.ds(pl.multiple_of(s * CAP, 16), CAP)
            rows = [
                jnp.sum(
                    p[CAP * i : CAP * i + CAP].astype(F32) * gg[i, at][:, :1],
                    axis=0,
                    keepdims=True,
                )
                for i in range(OWN)
            ]
            gg_o[s] = jnp.concatenate(rows + [jnp.zeros((8 - OWN, ROWS), F32)], axis=0)
            return carry

        lax.fori_loop(0, EP, back, 0)


def combine(part, gg, mg_o, gt_o, mine, buf, acc, m1, m2, m3, m3s, ls, ss, rs):
    d, e, z, c = place()
    greet(ep_peers(d, e))()
    send = Sender(ss, rs)
    right, left = (d, lax.rem(z + 1, CHIPS) * 2 + c), (d, lax.rem(z + 3, CHIPS) * 2 + c)
    other = (d, z * 2 + 1 - c)
    order = (2, 1, 3, 0)
    mates, locs = [], []
    for i, k in enumerate(order):
        t = lax.rem(z + k, CHIPS) * 2
        mates.append(send(part.at[t + 1 - c], buf.at[i], other))
        locs.append(pltpu.make_async_copy(part.at[t + c], mine.at[i], ls.at[i]))
        locs[i].start()
    rows = [send(gg.at[lax.rem(e + k, EP)], gt_o.at[e], (d, lax.rem(e + k, EP))) for k in range(1, EP)]

    def add(i):
        locs[i].wait()
        mates[i].wait_recv()
        for h in range(2):
            for q in range(2):
                r = slice(64 * q, 64 * q + 64)
                acc[i, h, r] = (
                    mine[i, pl.ds(128 * h + 64 * q, 64)].astype(F32)
                    + buf[i, pl.ds(128 * h + 64 * q, 64)].astype(F32)
                ).astype(BF)

    add(0)
    a = send(acc.at[0, 0], m1.at[0], right)
    b = send(acc.at[0, 1], m1.at[1], left)
    add(1)
    a2 = send(acc.at[1, 1], m2.at[0], right)
    add(2)
    b2 = send(acc.at[2, 0], m2.at[1], left)

    def pass_on(cp, i, h, slot, dev):
        cp.wait_recv()
        m3s[slot] = (acc[i, h].astype(F32) + m1[slot].astype(F32)).astype(BF)
        return send(m3s.at[slot], m3.at[slot], dev)

    a3 = pass_on(a, 1, 0, 0, right)
    b3 = pass_on(b, 2, 1, 1, left)
    add(3)
    own = pltpu.make_async_copy(gg.at[e], gt_o.at[e], ls.at[0])
    own.start()
    b2.wait_recv()
    a3.wait_recv()
    mg_o[:HALF] = acc[3, 0].astype(F32) + m2[1].astype(F32) + m3[0].astype(F32)
    a2.wait_recv()
    b3.wait_recv()
    mg_o[HALF:] = acc[3, 1].astype(F32) + m2[0].astype(F32) + m3[1].astype(F32)
    for cp in mates + [a, b, a2, b2, a3, b3]:
        cp.wait_send()
    for cp in rows:
        cp.wait()
    own.wait()


def norm_back(grad, values, factor, gain):
    scaled = grad * gain
    grad_gain = jnp.sum(grad * values * factor, axis=0, keepdims=True)
    mean = jnp.mean(scaled * values, axis=1, keepdims=True)
    return factor * (scaled - values * (factor * factor * mean)), grad_gain


def after_experts(mg, gg, rt, moe, mid, cot, gt, wo, out_o, gm_o, gb_o, da_o, st_o):
    m = mid[...]
    out_o[...] = (m + mg[:, :D]).astype(BF)
    router_t = gt[:EXPERTS].astype(BF)
    gates, _ = routing(rt, nt(router_t, moe[...]))
    back = gg[...][:, :OWN].reshape(EXPERTS, ROWS)
    both_ = gates * back
    gl = (both_ - gates * jnp.sum(both_, axis=0, keepdims=True)).astype(BF)
    st_o[...] = jnp.zeros_like(st_o)
    st_o[:EXPERTS] = nn(gl, moe[...])
    grad = mg[:, D:] + tn(gl, router_t)
    factor = lax.rsqrt(jnp.mean(m * m, axis=1, keepdims=True) + EPS)
    gm, gain = norm_back(grad, m, factor, gt[33:34])
    st_o[33:34] = gain
    gm = cot[...].astype(F32) + gm
    gm_o[...] = gm
    gb = (RES * gm).astype(BF)
    ga = nt(gb, wo[...]).astype(BF)
    for t in range(EP):
        gb_o[t] = gb[:, 128 * t : 128 * t + 128]
        da_o[t] = ga[:, 128 * t : 128 * t + 128]


def to_heads(da, gb, at, da_o, gb_o, at_o, ls, ss, rs):
    d, e, z, c = place()
    greet(ep_peers(d, e))()
    send = Sender(ss, rs)
    own = [
        pltpu.make_async_copy(da.at[e], da_o.at[e], ls.at[0]),
        pltpu.make_async_copy(gb.at[e], gb_o.at[e], ls.at[1]),
        pltpu.make_async_copy(at, at_o.at[e], ls.at[2]),
    ]
    for cp in own:
        cp.start()
    cps = []
    for k in (4, 3, 5, 2, 6, 1, 7):
        t = lax.rem(e + k, EP)
        cps.append(send(da.at[t], da_o.at[e], (d, t)))
        cps.append(send(gb.at[t], gb_o.at[e], (d, t)))
    start, finish = ring(at_o, d, e, z, c, send)
    a = start(at.at[0], at.at[1], 0)
    finish(a, start(at.at[0], at.at[1], 1))
    for cp in cps:
        cp.wait()
    for cp in own:
        cp.wait()


def attend_back(q, kv, nrm, att, lse, da, gb, at, cs, sn, ids, dq_o, dw_o, kk_s, vv_s, dk_s, dv_s):
    s = pl.program_id(0)
    kk_s[...], vv_s[...] = both(kv[0].astype(F32))
    dk_s[...] = jnp.zeros_like(dk_s)
    dv_s[...] = jnp.zeros_like(dv_s)
    ids_k = ids[0]
    ids_q = jnp.broadcast_to(ids_k, (128, LEN)).T[:, :1]
    low = lanes((ROWS, 128)) < HD

    def unturn(v, rows):
        return v * cs[rows] - turn(v) * sn[rows]

    dqs = []
    for i in range(4):
        rows = slice(ROWS * i, ROWS * i + ROWS)
        q2 = two_heads(q[0, rows].astype(F32)).astype(BF)
        o = da[2 * i : 2 * i + 2, 0].reshape(ROWS, 128).astype(F32)
        o2f = two_heads(o)
        o2 = o2f.astype(BF)
        a = att[2 * i : 2 * i + 2, 0].reshape(ROWS, 128).astype(F32)
        delta = jnp.sum(o2f * jnp.concatenate([a, a], axis=0), axis=1, keepdims=True)
        l2 = jnp.concatenate([lse[0, rows][:, :1], lse[0, rows][:, HD : HD + 1]], axis=0)
        own = ids_q[rows]
        own = jnp.concatenate([own, own], axis=0)
        at_, end = spans(i)
        dq = 0.0
        for span in ([slice(0, at_)] if at_ else []) + [slice(at_, end)]:
            t = nt(q2, kk_s[span]) * (SCORE * LOG2E) - l2
            if span.start == at_:
                t = jnp.where(ids_k[:, span] <= own, t, MASKED)
            p = jnp.exp2(t)
            gp = nt(o2, vv_s[span])
            ds = (p * (gp - delta)).astype(BF)
            dq = dq + nn(ds, kk_s[span])
            dk_s[span] += tn(ds, q2)
            dv_s[span] += tn(p.astype(BF), o2)
        dq = SCORE * jnp.where(low, dq[:ROWS], dq[ROWS:])
        dqs.append(unturn(dq, rows).astype(BF))
    w = []
    for i in range(4):
        rows = slice(ROWS * i, ROWS * i + ROWS)
        dk, dv = dk_s[rows], dv_s[rows]
        dk = unturn(SCORE * (dk + pltpu.roll(dk, HD, 1)), rows)
        dv = dv + pltpu.roll(dv, HD, 1)
        dkv = jnp.where(low, dk, dv).astype(BF)
        dqkv = jnp.concatenate([dqs[i], dkv], axis=1)
        dq_o[2 * i : 2 * i + 2, 0] = dqkv.reshape(2, HALF, 256)
        w.append(dqkv)
    wqkv = tn(nrm[0], jnp.concatenate(w, axis=0))
    wout = tn(at[:, 0].reshape(LEN, D), gb[:, 0].reshape(LEN, 128))
    w = jnp.concatenate([wqkv, wout], axis=1)

    @pl.when(s == 0)
    def _():
        dw_o[...] = w

    @pl.when(s == 1)
    def _():
        dw_o[...] += w


def to_tokens(dq, dq_o, ls, ss, rs):
    d, e, z, c = place()
    greet(ep_peers(d, e))()
    send = Sender(ss, rs)
    own = pltpu.make_async_copy(dq.at[e], dq_o.at[e], ls.at[0])
    own.start()
    cps = []
    for k in (4, 3, 5, 2, 6, 1, 7):
        t = lax.rem(e + k, EP)
        cps.append(send(dq.at[t], dq_o.at[e], (d, t)))
    for cp in cps:
        cp.wait()
    own.wait()


def first_norm_back(dq, wf, x, gm, gt, st, dw, gx_o, pk_o):
    grad = 0.0
    for s in range(EP):
        w = wf[s].astype(F32).reshape(D // 8, 16, 256)[:, :8].reshape(D, 256).astype(BF)
        grad = grad + nt(dq[s], w)
    v = x[...].astype(F32)
    factor = lax.rsqrt(jnp.mean(v * v, axis=1, keepdims=True) + EPS)
    g, gain = norm_back(grad, v, factor, gt[32:33])
    gx_o[...] = (gm[...] + g).astype(BF)
    row = lax.broadcasted_iota(jnp.int32, (128, D), 0)
    small = jnp.where(row == 32, gain, st[...]).T
    w = jnp.concatenate([dw[...], small], axis=1).astype(BF)
    pk_o[...] = w.reshape(DP, D // DP, 512)


def sum_weights(pk, wq_o, wk_o, wv_o, wo_o, sm_o, r1, s1, r2, ls, ss, rs):
    d, e, z, c = place()
    greet(ep_peers(d, e) + dp_peers(d, e))()
    send = Sender(ss, rs)
    own = pltpu.make_async_copy(pk.at[d], r1.at[d], ls.at[0])
    own.start()
    cps = [send(pk.at[p[0]], r1.at[d], p) for p in dp_peers(d, e)]
    own.wait()
    for cp in cps:
        cp.wait_recv()
    t = r1[0].astype(F32)
    for i in range(1, DP):
        t = t + r1[i].astype(F32)
    s1[...] = t.reshape(EP, 8, 512)
    own = pltpu.make_async_copy(s1.at[e], r2.at[e], ls.at[1])
    own.start()
    more = [send(s1.at[p[1]], r2.at[e], p) for p in ep_peers(d, e)]
    own.wait()
    for cp in more:
        cp.wait_recv()
    small = r2[0, :, 384:]
    for s in range(1, EP):
        small = small + r2[s, :, 384:]
    sm_o[...] = small
    wq_o[...] = jnp.concatenate([r2[s, :, :128] for s in range(EP)], axis=1)
    wk_o[...] = jnp.concatenate([r2[s, :, 128:192] for s in range(EP)], axis=1)
    wv_o[...] = jnp.concatenate([r2[s, :, 192:256] for s in range(EP)], axis=1)
    wo_o[...] = jnp.concatenate([r2[s, :, 256:384] for s in range(EP)], axis=1)
    for cp in cps + more:
        cp.wait_send()


def tables():
    even = np.arange(0, HD, 2).astype(np.float32)
    frequency = (np.float32(10000.0) ** (-even / np.float32(HD))).astype(np.float32)
    angle = np.arange(LEN, dtype=np.float32)[:, None] * frequency[None, :]
    angle = np.concatenate([angle] * 4, axis=1).astype(np.float64)
    return np.cos(angle).astype(np.float32), np.sin(angle).astype(np.float32)


def per_device(
    tokens, cotangent, block_ids, routes, w_query, w_key, w_value, w_output, w_router,
    gain_attn, gain_moe, expert_gate, expert_up, expert_down,
):
    x = tokens.reshape(ROWS, D)
    cot = cotangent.reshape(ROWS, D)
    rt = routes.reshape(ROWS, 8).T
    ids = block_ids.reshape(SEQS, 1, LEN)
    small = jnp.concatenate(
        [w_router, gain_attn[:, None], gain_moe[:, None], jnp.zeros((8, 222), BF)], axis=1
    )
    cos, sin = tables()
    cos, sin = jnp.asarray(cos), jnp.asarray(sin)
    params = pltpu.CompilerParams(vmem_limit_bytes=60 * MIB)
    once = pl.Buffered(1)

    def whole(shape):
        return pl.BlockSpec(shape, lambda s: (0,) * len(shape), pipeline_mode=once)

    xall, rall, wsl, wof = remote_call(
        gather_inputs, 1,
        [sds((EP, 2, HALF, D), BF), sds((EP, 8, ROWS), jnp.int32), sds((DP, EP, 16, 256), BF),
         sds((DP, EP, 16, 512), BF)],
        [tokens.reshape(2, HALF, D), rt, w_query, w_key, w_value, w_output, small],
        [ANY] + [VM] * 6,
        [pltpu.VMEM((EP, 16, 256), BF), pltpu.VMEM((16, 512), BF)],
        96,
    )
    cot_late, _ = lax.optimization_barrier((cot, xall))
    cot_all = lax.all_gather(cot_late, "ep", axis=0)

    seq = lambda *shape: pl.BlockSpec((1, *shape), lambda s: (s,) + (0,) * len(shape))
    cut = lambda n: pl.BlockSpec((EP, 1, HALF, n), lambda s: (0, s, 0, 0))
    q, kv, nrm, att, lse, gt, wo = pl.pallas_call(
        project_attend,
        name="project_attend",
        grid=(SEQS,),
        out_shape=[
            sds((SEQS, LEN, 128), BF), sds((SEQS, LEN, 128), BF), sds((SEQS, LEN, D), BF),
            sds((EP, 2, HALF, 128), BF), sds((SEQS, LEN, 128), F32), sds((128, D), F32),
            sds((D, D), BF),
        ],
        in_specs=[
            cut(D), whole((DP, EP, 16, 256)), whole((DP, EP, 16, 512)), whole((LEN, 128)),
            whole((LEN, 128)), seq(1, LEN),
        ],
        out_specs=[
            seq(LEN, 128), seq(LEN, 128), seq(LEN, D), cut(128), seq(LEN, 128), whole((128, D)),
            whole((D, D)),
        ],
        scratch_shapes=[
            pltpu.VMEM((D, 256), BF), pltpu.VMEM((LEN, 128), BF), pltpu.VMEM((LEN, 128), BF),
        ],
        compiler_params=params,
    )(xall, wsl, wof, cos, sin, ids)

    moe, mid, moe_own, at_own = remote_call(
        attended_to_moe, 2,
        [sds((EP, 2, HALF, D), BF), sds((ROWS, D), F32), sds((ROWS, D), BF), sds((ROWS, D), BF)],
        [att.reshape(EP, ROWS, 128), x, wo, gt],
        [ANY, VM, VM, VM],
        [pltpu.VMEM((EP, ROWS, 128), BF), pltpu.VMEM((2, HALF, D), BF)],
        24,
        [ANY, VM, VM, VM],
    )
    w_late, moe = lax.optimization_barrier((wsl, moe))
    w_full = lax.all_gather(w_late.reshape(D // 8, 16, 256), "ep", axis=0)

    each = lambda *shape: pl.BlockSpec((1, *shape), lambda j: (j,) + (0,) * len(shape))
    dw, hs, dg, du, gg, picks = pl.pallas_call(
        experts_weights,
        name="experts_weights",
        grid=(OWN,),
        out_shape=[
            sds((OWN, 3 * D, F), BF), sds((OWN, SLOTS, F), BF), sds((OWN, SLOTS, F), BF),
            sds((OWN, SLOTS, F), BF), sds((OWN, SLOTS, 128), F32), sds((EP, OWN * CAP, ROWS), BF),
        ],
        in_specs=[
            whole((EP, ROWS, D)), whole((EP, ROWS, D)), whole((EP, 8, ROWS)), whole((128, D)),
            each(D, F), each(D, F), each(F, D),
        ],
        out_specs=[
            each(3 * D, F), each(SLOTS, F), each(SLOTS, F), each(SLOTS, F), each(SLOTS, 128),
            whole((EP, OWN * CAP, ROWS)),
        ],
        scratch_shapes=[
            pltpu.VMEM((OWN, SLOTS, D), BF), pltpu.VMEM((OWN, SLOTS, D), BF),
            pltpu.VMEM((OWN, SLOTS, 128), F32),
        ],
        compiler_params=params,
    )(moe.reshape(EP, ROWS, D), cot_all, rall, gt, expert_gate, expert_up, expert_down)

    dw_sum = lax.psum(dw.reshape(OWN * 3 * D, F), "dp").reshape(OWN, 3 * D, F)

    part, gg_part = pl.pallas_call(
        experts_back,
        name="experts_back",
        grid=(OWN,),
        out_shape=[sds((EP, ROWS, 2 * D), BF), sds((EP, 8, ROWS), F32)],
        in_specs=[
            each(SLOTS, F), each(SLOTS, F), each(SLOTS, F), whole((OWN, SLOTS, 128)),
            whole((EP, OWN * CAP, ROWS)), each(D, F), each(D, F), each(F, D),
        ],
        out_specs=[whole((EP, ROWS, 2 * D)), whole((EP, 8, ROWS))],
        scratch_shapes=[pltpu.VMEM((EP, OWN * CAP, D), BF), pltpu.VMEM((EP, OWN * CAP, D), BF)],
        compiler_params=params,
    )(hs, dg, du, gg, picks, expert_gate, expert_up, expert_down)

    mg, gg_all = remote_call(
        combine, 3,
        [sds((ROWS, 2 * D), F32), sds((EP, 8, ROWS), F32)],
        [part, gg_part],
        [ANY, ANY],
        [
            pltpu.VMEM((4, ROWS, 2 * D), BF), pltpu.VMEM((4, ROWS, 2 * D), BF),
            pltpu.VMEM((4, 2, HALF, 2 * D), BF), pltpu.VMEM((2, HALF, 2 * D), BF),
            pltpu.VMEM((2, HALF, 2 * D), BF), pltpu.VMEM((2, HALF, 2 * D), BF),
            pltpu.VMEM((2, HALF, 2 * D), BF),
        ],
        20,
        [VM, ANY],
    )

    output, gm, gb, da, st = pl.pallas_call(
        after_experts,
        name="after_experts",
        out_shape=[
            sds((ROWS, D), BF), sds((ROWS, D), F32), sds((EP, ROWS, 128), BF),
            sds((EP, ROWS, 128), BF), sds((128, D), F32),
        ],
        in_specs=[VM] * 8,
        out_specs=[VM] * 5,
        compiler_params=params,
    )(mg, gg_all, rt, moe_own, mid, cot, gt, wo)

    da_all, gb_all, at_all = remote_call(
        to_heads, 4,
        [sds((EP, ROWS, 128), BF), sds((EP, ROWS, 128), BF), sds((EP, 2, HALF, D), BF)],
        [da, gb, at_own.reshape(2, HALF, D)],
        [ANY] * 3,
        [],
        32,
    )

    dq, dw_attn = pl.pallas_call(
        attend_back,
        name="attend_back",
        grid=(SEQS,),
        out_shape=[sds((EP, 2, HALF, 256), BF), sds((D, 384), F32)],
        in_specs=[
            seq(LEN, 128), seq(LEN, 128), seq(LEN, D), cut(128), seq(LEN, 128), cut(128),
            cut(128), cut(D), whole((LEN, 128)), whole((LEN, 128)), seq(1, LEN),
        ],
        out_specs=[cut(256), whole((D, 384))],
        scratch_shapes=[
            pltpu.VMEM((LEN, 128), BF), pltpu.VMEM((LEN, 128), BF),
            pltpu.VMEM((LEN, 128), F32), pltpu.VMEM((LEN, 128), F32),
        ],
        compiler_params=params,
    )(
        q, kv, nrm, att, lse, da_all.reshape(EP, 2, HALF, 128), gb_all.reshape(EP, 2, HALF, 128),
        at_all, cos, sin, ids,
    )

    (dq_all,) = remote_call(
        to_tokens, 5, [sds((EP, ROWS, 256), BF)], [dq.reshape(EP, ROWS, 256)], [ANY], [], 8
    )

    grad_x, packed = pl.pallas_call(
        first_norm_back,
        name="first_norm_back",
        out_shape=[sds((ROWS, D), BF), sds((DP, D // DP, 512), BF)],
        in_specs=[VM] * 7,
        out_specs=[VM] * 2,
        compiler_params=params,
    )(dq_all, w_full, x, gm, gt, st, dw_attn)

    gq, gk, gv, go, gs = remote_call(
        sum_weights, 6,
        [sds((8, D), F32), sds((8, 512), F32), sds((8, 512), F32), sds((8, D), F32), sds((8, 128), F32)],
        [packed],
        [ANY],
        [
            pltpu.VMEM((DP, D // DP, 512), BF), pltpu.VMEM((EP, 8, 512), F32),
            pltpu.VMEM((EP, 8, 512), F32),
        ],
        24,
        [VM] * 5,
    )

    f = dw_sum.astype(F32)
    down = jnp.concatenate([f[:, 2 * D : 2 * D + F], f[:, 2 * D + F :]], axis=2)
    return (
        output.reshape(tokens.shape),
        grad_x.reshape(tokens.shape),
        gq,
        gk,
        gv,
        go,
        gs[:, :EXPERTS],
        gs[:, 32],
        gs[:, 33],
        f[:, :D],
        f[:, D : 2 * D],
        down,
    )


def solution(mesh):
    rows, own, both_axes = P("dp", "ep", None), P("ep", None, None), P(("dp", "ep"), None)
    line = P(("dp", "ep"))
    return jax.shard_map(
        per_device,
        mesh=mesh,
        in_specs=(
            rows, rows, P("dp", None), rows, both_axes, both_axes, both_axes, both_axes, both_axes,
            line, line, own, own, own,
        ),
        out_specs=(
            rows, rows, both_axes, both_axes, both_axes, both_axes, both_axes, line, line, own,
            own, own,
        ),
        check_vma=False,
    )
```

time: 983 us -> 399 us (0.41)
  waiting for transfers between devices: 459 us -> 20.1 us
  Pallas kernels: 0 us -> 314 us
  local copies, waits for them, and re-layouts: 240 us -> 43.8 us
  matrix products: 137 us -> 0 us
  other arithmetic: 102 us -> 5.42 us
  starting transfers between devices: 22 us -> 0.3 us
    pallas_call x0 -> x12, Pallas kernels: none -> 314 us  [the longest x6 208 us: remote_call(): pl.pallas_call(body, name=body.__name__, out_shape=outs, in_specs=specs,...]
    dot_general x30 -> x0, matrix products: 137 us -> none  [the longest x1 11.7 us: per_device(): jnp.einsum('sqgrd,skgd->sgrqk', grad_att_grp, value_heads, preferred_elem...]
    unnamed x6 -> x3, waiting for transfers between devices: 135 us -> 0.05 us
    all_to_all x4 -> x0, waiting for transfers between devices: 130 us -> none  [the longest x1 51.1 us: per_device(): lax.all_to_all(grad_arrived, 'ep', split_axis=0, concat_axis=0, tiled=True)]
    psum x1, waiting for transfers between devices: 116 us -> 20 us  [per_device(): dw_sum = lax.psum(dw.reshape(OWN * 3 * D, F), 'dp').reshape(OWN, 3 * D, F)]
    all_gather x2, waiting for transfers between devices: 78.8 us -> 0.02 us  [the longest x1 0.02 us: per_device(): cot_all = lax.all_gather(cot_late, 'ep', axis=0)]
    gather x4 -> x0, local copies, waits for them, and re-layouts: 52.3 us -> none  [the longest x1 14.8 us: per_device(): grad_rows[assign_src].reshape(ep_size, local_experts, capacity, width)]
    convert_element_type x7 -> x0, local copies, waits for them, and re-layouts: 38.2 us -> none  [the longest x3 28.2 us: per_device(): part.astype(jnp.float32)]
  transfers between devices with their start and end apart: 9 -> 3, of which waited for: 8 -> 1; matrix products, arithmetic and copies ran while one was open for 30% -> 1% of each run, Pallas kernels for 0% -> 68%
where the time goes in v1:
time: 399 us; the launch traced here: 398 us
  Pallas kernels  314 us (79%)
  local copies, waits for them, and re-layouts  43.8 us (11%)
  waiting for transfers between devices  20.1 us (5%)
  between operations  13.9 us (3%)
  other arithmetic  5.42 us (1%)
    pallas_call x6, Pallas kernels, remote_call(): pl.pallas_call(body, name=body.__name__, out_shape=outs, in_specs=specs,...  208 us
    pallas_call x1, Pallas kernels, per_device(): pl.pallas_call(experts_weights, name='experts_weights', grid=(OWN,), out_...  33.9 us
    unnamed x53, local copies, waits for them, and re-layouts  24.9 us
    pallas_call x1, Pallas kernels, per_device(): pl.pallas_call(experts_back, name='experts_back', grid=(OWN,), out_shape=...  22.5 us
    pallas_call x1, Pallas kernels, per_device(): pl.pallas_call(attend_back, name='attend_back', grid=(SEQS,), out_shape=[...  20.2 us
    psum x1, waiting for transfers between devices, per_device(): dw_sum = lax.psum(dw.reshape(OWN * 3 * D, F), 'dp').reshape(OWN, 3 * D, F)  20 us
    pallas_call x1, Pallas kernels, per_device(): pl.pallas_call(project_attend, name='project_attend', grid=(SEQS,), out_s...  16 us
    slice x1, local copies, waits for them, and re-layouts, per_device(): f[:, D:2 * D]  12 us
  transfers between devices with their start and end apart: 3, of which 1 were waited for; matrix products, arithmetic and copies ran while one was open for 1% of the time, Pallas kernels for 68%

profile of v1, /device:TPU:1, one launch (start us, length us, event | category | flops | bytes accessed | tf_op | source)
XLA Modules:
  0.0 398.0 jit_solution(4397724724294048466)
XLA Ops:
  9.6 1.0 copy-done.2
  14.1 43.1 %gather_inputs.1 = (bf16[8,2,128,1024]{3,2,1,0:T(8,128)(2,1)}, s32[8,8,256]{2,1,0:T(8,128)S(1)}, bf16[16,8,16,256]{3,2,1,0:T(8,128)(2,1)}, bf16[16,8,16,512]{3,2,1,0:T(8,128)(2,1)S(1)}) custom-call(bf16[2,128,1024]{2,1,0:T(8,128)(2,1)S(1)} %copy-done.2, s32[8,256]{1,0:T(8,128)S(1)} %bitcast.27, bf16[8,1024]{1,0:T(8,128)(2,1)S(1)} %copy-done.20, ...), custom_call_target="tpu_custom_call" | custom-call | bytes 20971520 | tf_op jit(solution)/shard_map/gather_inputs/pallas_call | solution.py:120
  57.3 1.3 copy-done.5
  59.3 1.3 reshape.67.ids
  60.6 16.0 %project_attend.1 = (bf16[2,1024,128]{2,1,0:T(8,128)(2,1)}, bf16[2,1024,128]{2,1,0:T(8,128)(2,1)}, bf16[2,1024,1024]{2,1,0:T(8,128)(2,1)}, bf16[8,2,128,128]{3,2...) custom-call(bf16[8,2,128,1024]{3,2,1,0:T(8,128)(2,1)} %get-tuple-element.58.x, ...), custom_call_target="tpu_custom_call" | custom-call | tf_op jit(solution)/shard_map/project_attend/pallas_call | solution.py:696
  76.6 1.6 copy-done
  78.2 1.1 copy-done.1
  79.3 1.0 copy-done.6
  80.3 39.4 %attended_to_moe.1 = (bf16[8,2,128,1024]{3,2,1,0:T(8,128)(2,1)}, f32[256,1024]{1,0:T(8,128)S(1)}, bf16[256,1024]{1,0:T(8,128)(2,1)S(1)}, bf16[256,1024]{1,0:T(8,128)(2,1)S(1)}) custom-call(bf16[8,256,128]{2,1,0:T(8,128)(2,1)S(1)} %bitcast.20, bf16[256,1024]{1,0:T(8,128)(2,1)S(1)} %bitcast.19, bf16[1024,1024]{1,0:T(8,128)(2,1)S(1)} %copy-done, ...), custom_call_target="tpu_custom_call" | custom-call | bytes 20971520 | tf_op jit(solution)/shard_map/attended_to_moe/pallas_call | solution.py:120
  119.7 0.9 copy-done.10
  120.7 0.8 copy-done.15
  121.8 33.9 %experts_weights.1 = (bf16[4,3072,512]{2,1,0:T(8,128)(2,1)}, bf16[4,640,512]{2,1,0:T(8,128)(2,1)}, bf16[4,640,512]{2,1,0:T(8,128)(2,1)}, bf16[4,640,512]{2,1,0:T...) custom-call(bf16[8,256,1024]{2,1,0:T(8,128)(2,1)} %bitcast.29, bf16[8,256,1024]{2,1,0:T(8,128)(2,1)} %bitcast.28, ...), custom_call_target="tpu_custom_call" | custom-call | tf_op jit(solution)/shard_map/experts_weights/pallas_call | solution.py:732
  155.7 22.5 %experts_back.1 = (bf16[8,256,2048]{2,1,0:T(8,128)(2,1)}, f32[8,8,256]{2,1,0:T(8,128)}) custom-call(bf16[4,640,512]{2,1,0:T(8,128)(2,1)} %get-tuple-element.67.hs, bf16[4,640,512]{2,1,0:T(8,128)(2,1)} %get-tuple-element.68.dg, bf16[4,640,512]{2,1,0:T(8,128)(2,1)} %get-tuple-element.69.du, f32[4,640,128]{2,1,0:T(8,128)} %get-tuple-element.70.gg, ...), custom_call_target="tpu_custom_call" | custom-call | tf_op jit(solution)/shard_map/experts_back/pallas_call | solution.py:757
  178.2 0.8 copy-done.18
  179.1 41.2 %combine.1 = (f32[256,2048]{1,0:T(8,128)S(1)}, f32[8,8,256]{2,1,0:T(8,128)S(1)}) custom-call(bf16[8,256,2048]{2,1,0:T(8,128)(2,1)} %get-tuple-element.72.part, f32[8,8,256]{2,1,0:T(8,128)S(1)} %copy-done.18), custom_call_target="tpu_custom_call" | custom-call | bytes 20971520 | tf_op jit(solution)/shard_map/combine/pallas_call | solution.py:120
  220.3 1.3 copy-done.7
  222.3 6.1 %after_experts.1 = (bf16[256,1024]{1,0:T(8,128)(2,1)}, f32[256,1024]{1,0:T(8,128)}, bf16[8,256,128]{2,1,0:T(8,128)(2,1)}, bf16[8,256,128]{2,1,0:T(8,128)(2,1)}, f32[128,1024]{1,0:T(8,128)}) custom-call(f32[256,2048]{1,0:T(8,128)} %copy-done.7, f32[8,8,256]{2,1,0:T(8,128)} %copy-done.17, s32[8,256]{1,0:T(8,128)} %bitcast.26, bf16[256,1024]{1,0:T(8,128)(2,1)} %copy-done.15, ...), custom_call_target="tpu_custom_call" | custom-call | tf_op jit(solution)/shard_map/after_experts/pallas_call | solution.py:786
  228.4 1.1 copy-done.13
  229.4 1.0 copy-done.14
  230.5 36.2 %to_heads.1 = (bf16[8,256,128]{2,1,0:T(8,128)(2,1)S(1)}, bf16[8,256,128]{2,1,0:T(8,128)(2,1)S(1)}, bf16[8,2,128,1024]{3,2,1,0:T(8,128)(2,1)}) custom-call(bf16[8,256,128]{2,1,0:T(8,128)(2,1)S(1)} %copy-done.14, bf16[8,256,128]{2,1,0:T(8,128)(2,1)S(1)} %copy-done.13, bf16[2,128,1024]{2,1,0:T(8,128)(2,1)S(1)} %bitcast.22), custom_call_target="tpu_custom_call" | custom-call | bytes 20971520 | tf_op jit(solution)/shard_map/to_heads/pallas_call | solution.py:120
  266.8 0.8 copy-done.11
  268.3 20.2 %attend_back.1 = (bf16[8,2,128,256]{3,2,1,0:T(8,128)(2,1)}, f32[1024,384]{1,0:T(8,128)}) custom-call(bf16[2,1024,128]{2,1,0:T(8,128)(2,1)} %get-tuple-element.79.q, bf16[2,1024,128]{2,1,0:T(8,128)(2,1)} %get-tuple-element.80.kv, bf16[2,1024,1024]{2,1,0:T(8,128)(2,1)} %get-tuple-element.81.nrm, bf16[8,2,128,128]{3,2,1,0:T(8,128)(2,1)} %get-tuple-element.60.att, ...), custom_call_target="tpu_custom_call" | custom-call | tf_op jit(solution)/shard_map/attend_back/pallas_call | solution.py:807
  288.6 1.2 copy-done.8
  289.8 15.1 %to_tokens.1.dq = bf16[8,256,256]{2,1,0:T(8,128)(2,1)S(1)} custom-call(bf16[8,256,256]{2,1,0:T(8,128)(2,1)S(1)} %bitcast.21), custom_call_target="tpu_custom_call" | custom-call | bytes 20971520 | tf_op jit(solution)/shard_map/to_tokens/pallas_call | solution.py:120
  304.9 1.0 copy-done.4
  305.9 7.8 %first_norm_back.1 = (bf16[256,1024]{1,0:T(8,128)(2,1)}, bf16[16,64,512]{2,1,0:T(8,128)(2,1)}) custom-call(bf16[8,256,256]{2,1,0:T(8,128)(2,1)} %copy-done.4, bf16[8,128,16,256]{3,2,1,0:T(8,128)(2,1)} %all-gather.4.cloned.1.call-done.wf, bf16[256,1024]{1,0:T(8,128)(2,1)} %bitcast.18, f32[256,1024]{1,0:T(8,128)} %get-tuple-element.91.gm, ...), custom_call_target="tpu_custom_call" | custom-call | tf_op jit(solution)/shard_map/first_norm_back/pallas_call | solution.py:831
  313.7 1.2 copy-done.9
  314.9 32.7 %sum_weights.1 = (f32[8,1024]{1,0:T(8,128)S(1)}, f32[8,512]{1,0:T(8,128)S(1)}, f32[8,512]{1,0:T(8,128)S(1)}, f32[8,1024]{1,0:T(8,128)S(1)}, f32[8,128]{1,0:T(8,128)S(1)}) custom-call(bf16[16,64,512]{2,1,0:T(8,128)(2,1)S(1)} %copy-done.9), custom_call_target="tpu_custom_call" | custom-call | bytes 20971520 | tf_op jit(solution)/shard_map/sum_weights/pallas_call | solution.py:120
  348.4 20.0 %all-reduce.2.cloned.1.call-done = bf16[4,3072,512]{2,1,0:T(8,128)(2,1)} async-done(((bf16[4,3072,512]{2,1,0:T(8,128)(2,1)}), bf16[4,3072,512]{2,1,0:T(8,128)(2,1)}) %all-reduce.2.cloned.1.call-update) | async-done | bytes 12582928 | tf_op jit(solution)/shard_map/psum | solution.py:755
  368.4 3.4 fusion
  371.8 4.7 %pad_maximum_fusion = f32[4,512,1024]{2,1,0:T(8,128)} fusion(f32[4,512,512]{2,1,0:T(8,128)S(1)} %get-tuple-element.105, f32[4,512,512]{2,1,0:T(8,128)S(1)} %get-tuple-element.104), kind=kLoop, calls=%fused_computation | loop fusion | flops 2097152 | bytes 16777216 | tf_op jit(solution)/shard_map/concatenate | solution.py:854
  376.4 12.0 %fusion.1 = (f32[4,1024,512]{2,1,0:T(8,128)}, f32[4,1024,512]{2,1,0:T(8,128)}) fusion(bf16[4,3072,512]{2,1,0:T(8,128)(2,1)} %all-reduce.2.cloned.1.call-done), kind=kLoop, calls=%fused_computation.5 | loop fusion | bytes 33554432 | tf_op jit(solution)/shard_map/slice | solution.py:866
  (52 shorter events, 12.1 us)
Async XLA Ops:
  7.2 114.6 %all-gather.6.cloned.1.call-start = ((), (), s32[]{:S(2)}) async-start(), calls=%async_computation.2 | async-start | bytes 4718592 | tf_op jit(solution)/shard_map/all_gather | solution.py:692
  9.6 1.0 copy-start.2
  10.6 0.7 copy-start.19
  11.3 0.7 copy-start.20
  12.0 0.7 copy-start.21
  12.7 0.7 copy-start.22
  13.4 0.7 copy-start.23
  57.2 1.3 copy-start.5
  58.6 0.6 copy-start.16
  59.2 246.7 %all-gather.4.cloned.1.call-start = ((), (), s32[]{:S(2)}) async-start(), calls=%async_computation | async-start | bytes 9437184 | tf_op jit(solution)/shard_map/all_gather | solution.py:729
  60.6 16.0 %copy-start.3 = (bf16[2,128,1024]{2,1,0:T(8,128)(2,1)S(1)}, bf16[2,128,1024]{2,1,0:T(8,128)(2,1)}, u32[]{:S(2)}) copy-start(bf16[2,128,1024]{2,1,0:T(8,128)(2,1)} %x.1) | copy-start | bytes 1572868
  76.6 1.6 copy-start
  78.2 1.1 copy-start.1
  79.3 1.0 copy-start.6
  119.7 1.0 copy-start.10
  120.7 0.8 copy-start.15
  121.5 246.9 %all-reduce.2.cloned.1.call-start = ((), (), s32[]{:S(2)}) async-start(), calls=%async_computation.1 | async-start | bytes 25165824 | tf_op jit(solution)/shard_map/psum | solution.py:755
  178.2 0.8 copy-start.18
  220.3 1.3 copy-start.7
  221.6 0.6 copy-start.17
  228.4 1.1 copy-start.13
  229.4 1.0 copy-start.14
  266.7 0.8 copy-start.11
  267.6 0.8 copy-start.12
  288.6 1.2 copy-start.8
  304.9 1.0 copy-start.4
  313.7 1.2 copy-start.9
Sparse Core Ops, SparseCore 0:
  59.3 41.9 all-gather.5
  121.6 52.9 all-gather.3
  178.3 190.1 all-reduce.1

commit v2 on v1

--- a/solution.py
+++ b/solution.py
@@ -66,54 +66,55 @@
     def __call__(self, src, dst, dev):
         i = self.n
         self.n += 1
-        cp = pltpu.make_async_remote_copy(
+        return pltpu.make_async_remote_copy(
             src, dst, self.ss.at[i], self.rs.at[i], device_id=dev, device_id_type=MESH
         )
+
+    def now(self, src, dst, dev):
+        cp = self(src, dst, dev)
         cp.start()
         return cp
 
 
-def ring(out, d, e, z, c, send):
-    right, left = (d, lax.rem(z + 1, CHIPS) * 2 + c), (d, lax.rem(z + 3, CHIPS) * 2 + c)
-    part = (d, z * 2 + 1 - c)
-    er, el, eo = right[1], left[1], lax.rem(z + 2, CHIPS) * 2 + c
-
-    def start(src0, src1, half):
-        if half == 0:
-            return [
-                send(src0, out.at[e, 0], right),
-                send(src0, out.at[e, 0], left),
-                send(src0, out.at[e, 0], part),
-            ]
-        return [
-            send(src1, out.at[e, 1], left),
-            send(src1, out.at[e, 1], right),
-            send(src1, out.at[e, 1], part),
+class Ring:
+    def __init__(self, out, src0, src1, d, e, z, c, make):
+        right, left = (d, lax.rem(z + 1, CHIPS) * 2 + c), (d, lax.rem(z + 3, CHIPS) * 2 + c)
+        part = (d, z * 2 + 1 - c)
+        er, el, eo = right[1], left[1], lax.rem(z + 2, CHIPS) * 2 + c
+        self.near = [
+            [make(src0, out.at[e, 0], right), make(src0, out.at[e, 0], left)],
+            [make(src1, out.at[e, 1], left), make(src1, out.at[e, 1], right)],
         ]
-
-    def finish(a, b):
-        (r0, l0, p0), (l1, r1, p1) = a, b
-        f = []
-        r0.wait_recv()
-        fr = send(out.at[el, 0], out.at[el, 0], right)
-        f.append(send(out.at[el, 0], out.at[el, 0], part))
-        l1.wait_recv()
-        fl = send(out.at[er, 1], out.at[er, 1], left)
-        f.append(send(out.at[er, 1], out.at[er, 1], part))
-        r1.wait_recv()
-        f.append(send(out.at[el, 1], out.at[el, 1], part))
-        l0.wait_recv()
-        f.append(send(out.at[er, 0], out.at[er, 0], part))
-        fr.wait_recv()
-        f.append(send(out.at[eo, 0], out.at[eo, 0], part))
-        fl.wait_recv()
-        f.append(send(out.at[eo, 1], out.at[eo, 1], part))
-        for cp in (r0, l0, l1, r1, fr, fl):
+        self.mate = [make(src0, out.at[e, 0], part), make(src1, out.at[e, 1], part)]
+        self.far = [
+            make(out.at[el, 0], out.at[el, 0], right),
+            make(out.at[er, 1], out.at[er, 1], left),
+        ]
+        self.share = [make(out.at[s, h], out.at[s, h], part) for s, h in
+                      ((el, 0), (er, 1), (el, 1), (er, 0), (eo, 0), (eo, 1))]
+
+    def start(self, h):
+        for cp in self.near[h]:
+            cp.start()
+        self.mate[h].start()
+
+    def forward(self):
+        for h in range(2):
+            self.near[h][0].wait_recv()
+            self.far[h].start()
+            self.share[h].start()
+        for h in range(2):
+            self.near[1 - h][1].wait_recv()
+            self.share[2 + h].start()
+
+    def finish(self):
+        for h in range(2):
+            self.far[h].wait_recv()
+            self.share[4 + h].start()
+        for cp in self.near[0] + self.near[1] + self.far:
             cp.wait_send()
-        for cp in [p0, p1] + f:
+        for cp in self.mate + self.share:
             cp.wait()
-
-    return start, finish
 
 
 def remote_call(body, cid, outs, ins, specs, scratch, sems, out_specs=None, vmem=48, flops=0):
@@ -140,63 +141,64 @@
     return jax.ShapeDtypeStruct(shape, dtype)
 
 
-def gather_inputs(x, rt, wq, wk, wv, wo, sm, xall, rall, wsl, wof, wp, wop, ls, ss, rs):
+def gather_inputs(x, rt, wq, wo, sm, xall, rall, wsl, wof, wp, wop, ls, ss, rs):
     d, e, z, c = place()
-    wait = greet(ep_peers(d, e) + dp_peers(d, e))
-    q, k, v = wq[...].astype(F32), wk[...].astype(F32), wv[...].astype(F32)
+    u, v = d // 4, lax.rem(d, 4)
+    across = [(lax.rem(u + k, 4) * 4 + v, e) for k in (1, 3, 2)]
+    along = [(u * 4 + lax.rem(v + k, 4), e) for k in (1, 3, 2)]
+    wait = greet(ep_peers(d, e) + across + along)
+    q = wq[...].astype(F32)
     small = sm[...].astype(F32)
     for t in range(EP):
-        row = jnp.concatenate(
-            [
-                q[:, 128 * t : 128 * t + 128],
-                k[:, 64 * t : 64 * t + 64],
-                v[:, 64 * t : 64 * t + 64],
-            ],
-            axis=1,
-        )
-        wp[t] = jnp.concatenate([row, small], axis=0).astype(BF)
+        wp[t] = jnp.concatenate([q[:, 256 * t : 256 * t + 256], small], axis=0).astype(BF)
     o = wo[...].astype(F32)
     wop[...] = jnp.concatenate([o[:, :512], o[:, 512:]], axis=0).astype(BF)
     wait()
-    send = Sender(ss, rs)
+    make = Sender(ss, rs)
+    send = make.now
     own = [
         pltpu.make_async_copy(x, xall.at[e], ls.at[0]),
-        pltpu.make_async_copy(wp.at[e], wsl.at[d, e], ls.at[1]),
-        pltpu.make_async_copy(wop, wof.at[d, e], ls.at[2]),
+        pltpu.make_async_copy(wp.at[e], wsl.at[v, u, e], ls.at[1]),
+        pltpu.make_async_copy(wop, wof.at[u, v, e], ls.at[2]),
         pltpu.make_async_copy(rt, rall.at[e], ls.at[3]),
     ]
     for cp in own:
         cp.start()
-    first = []
-    for k in range(1, EP):
-        t = lax.rem(e + k, EP)
-        first.append(send(wp.at[t], wsl.at[d, e], (d, t)))
-    for k in range(1, EP):
-        t = lax.rem(e + k, EP)
-        first.append(send(wop, wof.at[d, e], (d, t)))
-    start, finish = ring(xall, d, e, z, c, send)
-    a = start(x.at[0], x.at[1], 0)
-    b = start(x.at[0], x.at[1], 1)
+    first = [send(wp.at[p[1]], wsl.at[v, u, e], p) for p in ep_peers(d, e)]
+    first += [send(wop, wof.at[u, v, e], p) for p in ep_peers(d, e)]
+    ring = Ring(xall, x.at[0], x.at[1], d, e, z, c, make)
+    ring.start(0)
+    ring.start(1)
     routes = [send(rt, rall.at[e], p) for p in ep_peers(d, e)]
     own[1].wait()
     for cp in first[: EP - 1]:
         cp.wait_recv()
-    second = [send(wsl.at[d], wsl.at[d], p) for p in dp_peers(d, e)]
+    w1 = [send(wsl.at[v, u], wsl.at[v, u], p) for p in across]
     own[2].wait()
     for cp in first[EP - 1 :]:
         cp.wait_recv()
     mine = pl.ds(c * 4, 4)
-    third = [send(wof.at[d, mine], wof.at[d, mine], p) for p in dp_peers(d, e)]
-    finish(a, b)
     part = (d, z * 2 + 1 - c)
+    o1 = [send(wof.at[u, v, mine], wof.at[u, v, mine], p) for p in along]
+    for cp in w1:
+        cp.wait_recv()
+    w2 = [send(wsl.at[v], wsl.at[v], p) for p in along]
+    for cp in o1:
+        cp.wait_recv()
+    o2 = [send(wof.at[u, :, mine], wof.at[u, :, mine], p) for p in across]
+    ring.forward()
+    ring.finish()
     last = []
-    for k, cp in enumerate(third):
+    for k, cp in zip((1, 3, 2), o1):
+        t = lax.rem(v + 4 - k, 4)
+        last.append(send(wof.at[u, t, mine], wof.at[u, t, mine], part))
+    for k, cp in zip((1, 3, 2), o2):
         cp.wait_recv()
-        s = lax.rem(d + DP - 1 - k, DP)
-        last.append(send(wof.at[s, mine], wof.at[s, mine], part))
-    for cp in first + third:
+        t = lax.rem(u + 4 - k, 4)
+        last.append(send(wof.at[t, :, mine], wof.at[t, :, mine], part))
+    for cp in first + w1 + o1 + o2:
         cp.wait_send()
-    for cp in routes + second + last:
+    for cp in routes + w2 + last:
         cp.wait()
     own[0].wait()
     own[3].wait()
@@ -228,15 +230,18 @@
 
 
 def project_attend(
-    x, wsl, wof, cs, sn, ids, q_o, kv_o, nrm_o, att_o, lse_o, gt_o, wo_o, w_s, kk_s, vv_s
+    x, wsl, wof, cs, sn, ids, q_o, kv_o, nrm_o, att_o, lse_o, gt_o, wo_o, w_s, sm_s, kk_s, vv_s
 ):
     @pl.when(pl.program_id(0) == 0)
     def _():
-        w = wsl[...].astype(F32).reshape(D // 8, 16, 256)
-        w_s[...] = w[:, :8].reshape(D, 256).astype(BF)
-        gt_o[...] = w[:, 8:].reshape(D, 256)[:, :128].T
+        for i in range(DP):
+            w = wsl[i % 4, i // 4].astype(F32)
+            rows = slice(64 * i, 64 * i + 64)
+            w_s[rows] = w[:, :8].reshape(64, 256).astype(BF)
+            sm_s[rows] = w[:, 8:, :128].reshape(64, 128)
+        gt_o[...] = sm_s[...].T
         for i in range(4):
-            o = wof[4 * i : 4 * i + 4].astype(F32).reshape(32, 16, 512)
+            o = wof[i].astype(F32).reshape(32, 16, 512)
             wo_o[256 * i : 256 * i + 256, :512] = o[:, :8].reshape(256, 512).astype(BF)
             wo_o[256 * i : 256 * i + 256, 512:] = o[:, 8:].reshape(256, 512).astype(BF)
 
@@ -285,7 +290,8 @@
 def attended_to_moe(att, x, wo, gt, moe, mid_o, own_o, at_o, arr, mo, ls, ss, rs):
     d, e, z, c = place()
     greet(ep_peers(d, e))()
-    send = Sender(ss, rs)
+    make = Sender(ss, rs)
+    send = make.now
     lc = pltpu.make_async_copy(att.at[e], arr.at[e], ls.at[0])
     lc.start()
     cps = []
@@ -295,9 +301,9 @@
     lc.wait()
     for cp in cps:
         cp.wait_recv()
-    start, finish = ring(moe, d, e, z, c, send)
+    ring = Ring(moe, mo.at[0], mo.at[1], d, e, z, c, make)
     gain = gt[33:34, :]
-    begun, own = [], []
+    own = []
     for h in range(2):
         rows = slice(HALF * h, HALF * h + HALF)
         a = jnp.concatenate([arr[s, rows] for s in range(EP)], axis=1)
@@ -310,8 +316,9 @@
         own_o[rows] = n
         own.append(pltpu.make_async_copy(mo.at[h], moe.at[e, h], ls.at[1 + h]))
         own[h].start()
-        begun.append(start(mo.at[0], mo.at[1], h))
-    finish(*begun)
+        ring.start(h)
+    ring.forward()
+    ring.finish()
     for cp in cps:
         cp.wait_send()
     for cp in own:
@@ -388,90 +395,193 @@
     dw_o[0, 2 * D + F :] = w[:, F:].astype(BF)
 
 
-def experts_back(hs, dg, du, gg, picks, wg, wu, wd, part_o, gg_o, eo_s, dx_s):
+class Reduce:
+    def __init__(self, chunk, me, ahead, behind, one, two, three, make):
+        at = lambda k: lax.rem(me + k, 4)
+        self.one, self.two, self.three = one, two, three
+        self.first = [
+            make(chunk(at(2), 0), one.at[0], ahead),
+            make(chunk(at(2), 1), one.at[1], behind),
+        ]
+        self.second = [
+            make(chunk(at(1), 1), two.at[0], ahead),
+            make(chunk(at(3), 0), two.at[1], behind),
+        ]
+        self.third = [make(one.at[0], three.at[0], ahead), make(one.at[1], three.at[1], behind)]
+
+    def start(self):
+        for cp in self.first + self.second:
+            cp.start()
+
+    def go_on(self, k, mine, pieces):
+        self.first[k].wait_recv()
+
+        def add(i, carry):
+            self.one[k, i] = self.one[k, i] + mine[i]
+            return carry
+
+        lax.fori_loop(0, pieces, add, 0)
+        self.third[k].start()
+
+    def arrived(self, k):
+        self.second[1 - k].wait_recv()
+        self.third[k].wait_recv()
+
+    def sent(self):
+        for cp in self.first + self.second + self.third:
+            cp.wait_send()
+
+
+def experts_combine(
+    hs, dg, du, gg, picks, wg, wu, wd, dw, at, mg_o, gt_o, at_o, sh_o,
+    eo_s, dx_s, gg_s, stage, buf, m1, m2, m3,
+    a1, a2, a3, amine, ac, b1, b2, b3, bmine, bc, a4, a5, a6, b4, b5, b6, ls, ss, rs,
+):
     j = pl.program_id(0)
+    d, e, z, c = place()
+    u, v = d // 4, lax.rem(d, 4)
+    near = lambda k, n: lax.rem(k + n, 4)
+    up, down = (near(u, 1) * 4 + v, e), (near(u, 3) * 4 + v, e)
+    ahead, behind = (u * 4 + near(v, 1), e), (u * 4 + near(v, 3), e)
+    right, left = (d, near(z, 1) * 2 + c), (d, near(z, 3) * 2 + c)
+    other = (d, z * 2 + 1 - c)
+    make = Sender(ss, rs)
+    ring = Ring(at_o, at.at[0], at.at[1], d, e, z, c, make)
+    half = lambda h: pl.ds(2 * h, 2)
+    deep = lambda h: pl.ds(48 * h, 48)
+    ra = Reduce(lambda i, h: dw.at[:, i, half(h), 0], u, up, down, a1, a2, a3, make)
+    rb = Reduce(lambda i, h: dw.at[:, half(h), i, 1], v, ahead, behind, b1, b2, b3, make)
+    qa = Reduce(lambda i, h: ac.at[:, i, deep(h)], v, ahead, behind, a4, a5, a6, make)
+    qb = Reduce(lambda i, h: bc.at[:, i, deep(h)], u, up, down, b4, b5, b6, make)
+    load = pltpu.make_async_copy
+    own = [
+        load(dw.at[:, near(u, 1), half(0), 0], amine.at[0], ls.at[0]),
+        load(dw.at[:, near(u, 3), half(1), 0], amine.at[1], ls.at[1]),
+        load(dw.at[:, half(0), near(v, 1), 1], bmine.at[0], ls.at[2]),
+        load(dw.at[:, half(1), near(v, 3), 1], bmine.at[1], ls.at[3]),
+        load(dw.at[:, u, :, 0], ac, ls.at[4]),
+        load(dw.at[:, :, v, 1], bc, ls.at[5]),
+        load(at, at_o.at[e], ls.at[6]),
+    ]
+
+    @pl.when(j == 0)
+    def _():
+        greet(ep_peers(d, e) + [up, down, ahead, behind])()
+        ra.start()
+        rb.start()
+        ring.start(0)
+        ring.start(1)
+        for cp in own:
+            cp.start()
+
     eo = nn(hs[0], wd[0]).astype(BF)
     dx = (nt(dg[0], wg[0]) + nt(du[0], wu[0])).astype(BF)
     for s in range(EP):
-        eo_s[s, pl.ds(pl.multiple_of(j * CAP, 16), CAP)] = eo[CAP * s : CAP * s + CAP]
-        dx_s[s, pl.ds(pl.multiple_of(j * CAP, 16), CAP)] = dx[CAP * s : CAP * s + CAP]
+        row = pl.ds(pl.multiple_of(j * CAP, 16), CAP)
+        eo_s[s, row] = eo[CAP * s : CAP * s + CAP]
+        dx_s[s, row] = dx[CAP * s : CAP * s + CAP]
+
+    @pl.when(j == 2)
+    def _():
+        ring.forward()
 
     @pl.when(j == OWN - 1)
     def _():
-        def back(s, carry):
+        for cp in own:
+            cp.wait()
+        for k in range(2):
+            ra.go_on(k, amine.at[k], OWN)
+            rb.go_on(k, bmine.at[k], OWN)
+
+        def gate_rows(s):
             p = picks[s]
-            part_o[s, :, :D] = tn(p, eo_s[s]).astype(BF)
-            part_o[s, :, D:] = tn(p, dx_s[s]).astype(BF)
-            at = pl.ds(pl.multiple_of(s * CAP, 16), CAP)
+            row = pl.ds(pl.multiple_of(s * CAP, 16), CAP)
             rows = [
                 jnp.sum(
-                    p[CAP * i : CAP * i + CAP].astype(F32) * gg[i, at][:, :1],
-                    axis=0,
-                    keepdims=True,
+                    p[CAP * i : CAP * i + CAP].astype(F32) * gg[i, row][:, :1], axis=0, keepdims=True
                 )
                 for i in range(OWN)
             ]
-            gg_o[s] = jnp.concatenate(rows + [jnp.zeros((8 - OWN, ROWS), F32)], axis=0)
-            return carry
-
-        lax.fori_loop(0, EP, back, 0)
-
-
-def combine(part, gg, mg_o, gt_o, mine, buf, acc, m1, m2, m3, m3s, ls, ss, rs):
-    d, e, z, c = place()
-    greet(ep_peers(d, e))()
-    send = Sender(ss, rs)
-    right, left = (d, lax.rem(z + 1, CHIPS) * 2 + c), (d, lax.rem(z + 3, CHIPS) * 2 + c)
-    other = (d, z * 2 + 1 - c)
-    order = (2, 1, 3, 0)
-    mates, locs = [], []
-    for i, k in enumerate(order):
-        t = lax.rem(z + k, CHIPS) * 2
-        mates.append(send(part.at[t + 1 - c], buf.at[i], other))
-        locs.append(pltpu.make_async_copy(part.at[t + c], mine.at[i], ls.at[i]))
-        locs[i].start()
-    rows = [send(gg.at[lax.rem(e + k, EP)], gt_o.at[e], (d, lax.rem(e + k, EP))) for k in range(1, EP)]
-
-    def add(i):
-        locs[i].wait()
-        mates[i].wait_recv()
-        for h in range(2):
-            for q in range(2):
-                r = slice(64 * q, 64 * q + 64)
-                acc[i, h, r] = (
-                    mine[i, pl.ds(128 * h + 64 * q, 64)].astype(F32)
-                    + buf[i, pl.ds(128 * h + 64 * q, 64)].astype(F32)
-                ).astype(BF)
-
-    add(0)
-    a = send(acc.at[0, 0], m1.at[0], right)
-    b = send(acc.at[0, 1], m1.at[1], left)
-    add(1)
-    a2 = send(acc.at[1, 1], m2.at[0], right)
-    add(2)
-    b2 = send(acc.at[2, 0], m2.at[1], left)
-
-    def pass_on(cp, i, h, slot, dev):
-        cp.wait_recv()
-        m3s[slot] = (acc[i, h].astype(F32) + m1[slot].astype(F32)).astype(BF)
-        return send(m3s.at[slot], m3.at[slot], dev)
-
-    a3 = pass_on(a, 1, 0, 0, right)
-    b3 = pass_on(b, 2, 1, 1, left)
-    add(3)
-    own = pltpu.make_async_copy(gg.at[e], gt_o.at[e], ls.at[0])
-    own.start()
-    b2.wait_recv()
-    a3.wait_recv()
-    mg_o[:HALF] = acc[3, 0].astype(F32) + m2[1].astype(F32) + m3[0].astype(F32)
-    a2.wait_recv()
-    b3.wait_recv()
-    mg_o[HALF:] = acc[3, 1].astype(F32) + m2[0].astype(F32) + m3[1].astype(F32)
-    for cp in mates + [a, b, a2, b2, a3, b3]:
-        cp.wait_send()
-    for cp in rows:
-        cp.wait()
-    own.wait()
+            gg_s[s] = jnp.concatenate(rows + [jnp.zeros((8 - OWN, ROWS), F32)], axis=0)
+
+        turns = [near(z, k) * 2 for k in (2, 1, 3, 0)]
+        mates = []
+        for i, t in enumerate(turns):
+            s = t + 1 - c
+            stage[i, :, :D] = tn(picks[s], eo_s[s]).astype(BF)
+            stage[i, :, D:] = tn(picks[s], dx_s[s]).astype(BF)
+            mates.append(make.now(stage.at[i], buf.at[i], other))
+        ring.finish()
+
+        def add(i):
+            s = turns[i] + c
+            left_, right_ = tn(picks[s], eo_s[s]), tn(picks[s], dx_s[s])
+            mates[i].wait_recv()
+            buf[i, :, :D] = (buf[i, :, :D].astype(F32) + left_).astype(BF)
+            buf[i, :, D:] = (buf[i, :, D:].astype(F32) + right_).astype(BF)
+
+        lo, hi = slice(0, HALF), slice(HALF, ROWS)
+        add(0)
+        s1 = [make.now(buf.at[0, pl.ds(0, HALF)], m1.at[0], right)]
+        s1.append(make.now(buf.at[0, pl.ds(HALF, HALF)], m1.at[1], left))
+        add(1)
+        s2 = [make.now(buf.at[1, pl.ds(HALF, HALF)], m2.at[0], right)]
+        add(2)
+        s2.append(make.now(buf.at[2, pl.ds(0, HALF)], m2.at[1], left))
+        for s in range(EP):
+            gate_rows(s)
+        rows = [make.now(gg_s.at[p[1]], gt_o.at[e], p) for p in ep_peers(d, e)]
+        gt_own = load(gg_s.at[e], gt_o.at[e], ls.at[7])
+        gt_own.start()
+        s1[0].wait_recv()
+        m1[0] = m1[0] + buf[1, lo]
+        s3 = [make.now(m1.at[0], m3.at[0], right)]
+        s1[1].wait_recv()
+        m1[1] = m1[1] + buf[2, hi]
+        s3.append(make.now(m1.at[1], m3.at[1], left))
+        add(3)
+
+        def close(r, chunk):
+            for k in range(2):
+                r.arrived(k)
+
+                def body(i, carry):
+                    for q in range(2):
+                        piece = r.two[1 - k, i, q].astype(F32) + r.three[k, i, q].astype(F32)
+                        chunk[i, 2 * k + q] = (chunk[i, 2 * k + q].astype(F32) + piece).astype(BF)
+                    return carry
+
+                lax.fori_loop(0, OWN, body, 0)
+
+        close(ra, ac)
+        qa.start()
+        close(rb, bc)
+        qb.start()
+        s2[1].wait_recv()
+        s3[0].wait_recv()
+        mg_o[lo] = buf[3, lo].astype(F32) + m2[1].astype(F32) + m3[0].astype(F32)
+        s2[0].wait_recv()
+        s3[1].wait_recv()
+        mg_o[hi] = buf[3, hi].astype(F32) + m2[0].astype(F32) + m3[1].astype(F32)
+        for q, chunk, me in ((qa, ac, v), (qb, bc, u)):
+            for k in range(2):
+                t = near(me, 1 + 2 * k)
+                q.first[k].wait_recv()
+                q.one[k] = q.one[k] + chunk[:, t, 48 * k : 48 * k + 48]
+                q.third[k].start()
+        for h, q, chunk, me in ((0, qa, ac, v), (1, qb, bc, u)):
+            for k in range(2):
+                q.arrived(k)
+                mine = chunk[:, me, 48 * k : 48 * k + 48].astype(F32)
+                total = mine + q.two[1 - k].astype(F32) + q.three[k].astype(F32)
+                sh_o[:, h, 48 * k : 48 * k + 48] = total.astype(BF)
+        for r in (ra, rb, qa, qb):
+            r.sent()
+        for cp in mates + s1 + s2 + s3:
+            cp.wait_send()
+        for cp in rows:
+            cp.wait()
+        gt_own.wait()
 
 
 def norm_back(grad, values, factor, gain):
@@ -504,14 +614,14 @@
         da_o[t] = ga[:, 128 * t : 128 * t + 128]
 
 
-def to_heads(da, gb, at, da_o, gb_o, at_o, ls, ss, rs):
+def to_heads(da, gb, da_o, gb_o, ls, ss, rs):
     d, e, z, c = place()
     greet(ep_peers(d, e))()
-    send = Sender(ss, rs)
+    make = Sender(ss, rs)
+    send = make.now
     own = [
         pltpu.make_async_copy(da.at[e], da_o.at[e], ls.at[0]),
         pltpu.make_async_copy(gb.at[e], gb_o.at[e], ls.at[1]),
-        pltpu.make_async_copy(at, at_o.at[e], ls.at[2]),
     ]
     for cp in own:
         cp.start()
@@ -520,9 +630,6 @@
         t = lax.rem(e + k, EP)
         cps.append(send(da.at[t], da_o.at[e], (d, t)))
         cps.append(send(gb.at[t], gb_o.at[e], (d, t)))
-    start, finish = ring(at_o, d, e, z, c, send)
-    a = start(at.at[0], at.at[1], 0)
-    finish(a, start(at.at[0], at.at[1], 1))
     for cp in cps:
         cp.wait()
     for cp in own:
@@ -593,7 +700,8 @@
 def to_tokens(dq, dq_o, ls, ss, rs):
     d, e, z, c = place()
     greet(ep_peers(d, e))()
-    send = Sender(ss, rs)
+    make = Sender(ss, rs)
+    send = make.now
     own = pltpu.make_async_copy(dq.at[e], dq_o.at[e], ls.at[0])
     own.start()
     cps = []
@@ -608,36 +716,60 @@
 def first_norm_back(dq, wf, x, gm, gt, st, dw, gx_o, pk_o):
     grad = 0.0
     for s in range(EP):
-        w = wf[s].astype(F32).reshape(D // 8, 16, 256)[:, :8].reshape(D, 256).astype(BF)
-        grad = grad + nt(dq[s], w)
+        grad = grad + nt(dq[s], wf[:, 256 * s : 256 * s + 256])
     v = x[...].astype(F32)
     factor = lax.rsqrt(jnp.mean(v * v, axis=1, keepdims=True) + EPS)
     g, gain = norm_back(grad, v, factor, gt[32:33])
     gx_o[...] = (gm[...] + g).astype(BF)
     row = lax.broadcasted_iota(jnp.int32, (128, D), 0)
     small = jnp.where(row == 32, gain, st[...]).T
-    w = jnp.concatenate([dw[...], small], axis=1).astype(BF)
-    pk_o[...] = w.reshape(DP, D // DP, 512)
-
-
-def sum_weights(pk, wq_o, wk_o, wv_o, wo_o, sm_o, r1, s1, r2, ls, ss, rs):
+    pk_o[0] = dw[:, :256].astype(BF).reshape(4, 4, 64, 256)
+    w = jnp.concatenate([dw[:, 256:], small], axis=1).astype(BF)
+    pk_o[1] = w.reshape(4, 4, 64, 256)
+
+
+def sum_weights(pk, wq_o, wk_o, wv_o, wo_o, sm_o, ra, rb, ta, tb, qa, qb, s1, r2, ls, ss, rs):
     d, e, z, c = place()
-    greet(ep_peers(d, e) + dp_peers(d, e))()
-    send = Sender(ss, rs)
-    own = pltpu.make_async_copy(pk.at[d], r1.at[d], ls.at[0])
-    own.start()
-    cps = [send(pk.at[p[0]], r1.at[d], p) for p in dp_peers(d, e)]
-    own.wait()
-    for cp in cps:
+    u, v = d // 4, lax.rem(d, 4)
+    across = [(lax.rem(u + k, 4) * 4 + v, e) for k in (1, 3, 2)]
+    along = [(u * 4 + lax.rem(v + k, 4), e) for k in (1, 3, 2)]
+    greet(ep_peers(d, e) + across + along)()
+    make = Sender(ss, rs)
+    send = make.now
+    own = [
+        pltpu.make_async_copy(pk.at[0, u], ra.at[0], ls.at[0]),
+        pltpu.make_async_copy(pk.at[1, :, v], rb.at[0], ls.at[1]),
+    ]
+    for cp in own:
+        cp.start()
+    a1, b1 = [], []
+    for i, k in enumerate((1, 3, 2)):
+        a1.append(send(pk.at[0, lax.rem(u + k, 4)], ra.at[1 + i], across[i]))
+        b1.append(send(pk.at[1, :, lax.rem(v + k, 4)], rb.at[1 + i], along[i]))
+    for cp in own:
+        cp.wait()
+
+    def total(r):
+        return (r[0].astype(F32) + r[1].astype(F32)) + (r[2].astype(F32) + r[3].astype(F32))
+
+    for cp in a1:
         cp.wait_recv()
-    t = r1[0].astype(F32)
-    for i in range(1, DP):
-        t = t + r1[i].astype(F32)
-    s1[...] = t.reshape(EP, 8, 512)
-    own = pltpu.make_async_copy(s1.at[e], r2.at[e], ls.at[1])
-    own.start()
+    ta[...] = total(ra).astype(BF)
+    a2 = [send(ta.at[lax.rem(v + k, 4)], qa.at[1 + i], along[i]) for i, k in enumerate((1, 3, 2))]
+    qa[0] = ta[v]
+    for cp in b1:
+        cp.wait_recv()
+    tb[...] = total(rb).astype(BF)
+    b2 = [send(tb.at[lax.rem(u + k, 4)], qb.at[1 + i], across[i]) for i, k in enumerate((1, 3, 2))]
+    qb[0] = tb[u]
+    for cp in a2:
+        cp.wait_recv()
+    s1[:, :, :256] = total(qa).reshape(EP, 8, 256)
+    for cp in b2:
+        cp.wait_recv()
+    s1[:, :, 256:] = total(qb).reshape(EP, 8, 256)
+    r2[e] = s1[e]
     more = [send(s1.at[p[1]], r2.at[e], p) for p in ep_peers(d, e)]
-    own.wait()
     for cp in more:
         cp.wait_recv()
     small = r2[0, :, 384:]
@@ -648,8 +780,16 @@
     wk_o[...] = jnp.concatenate([r2[s, :, 128:192] for s in range(EP)], axis=1)
     wv_o[...] = jnp.concatenate([r2[s, :, 192:256] for s in range(EP)], axis=1)
     wo_o[...] = jnp.concatenate([r2[s, :, 256:384] for s in range(EP)], axis=1)
-    for cp in cps + more:
+    for cp in a1 + b1 + a2 + b2 + more:
         cp.wait_send()
+
+
+def widen(dw, g_o, u_o, d_o):
+    w = dw[...].reshape(3 * D, F).astype(F32)
+    g_o[0] = w[:D]
+    u_o[0] = w[D : 2 * D]
+    d_o[0, :, :F] = w[2 * D : 2 * D + F]
+    d_o[0, :, F:] = w[2 * D + F :]
 
 
 def tables():
@@ -671,6 +811,9 @@
     small = jnp.concatenate(
         [w_router, gain_attn[:, None], gain_moe[:, None], jnp.zeros((8, 222), BF)], axis=1
     )
+    w_qkv = jnp.concatenate(
+        [w_query.reshape(8, EP, 128), w_key.reshape(8, EP, HD), w_value.reshape(8, EP, HD)], axis=2
+    ).reshape(8, 2 * D)
     cos, sin = tables()
     cos, sin = jnp.asarray(cos), jnp.asarray(sin)
     params = pltpu.CompilerParams(vmem_limit_bytes=60 * MIB)
@@ -681,15 +824,18 @@
 
     xall, rall, wsl, wof = remote_call(
         gather_inputs, 1,
-        [sds((EP, 2, HALF, D), BF), sds((EP, 8, ROWS), jnp.int32), sds((DP, EP, 16, 256), BF),
-         sds((DP, EP, 16, 512), BF)],
-        [tokens.reshape(2, HALF, D), rt, w_query, w_key, w_value, w_output, small],
-        [ANY] + [VM] * 6,
+        [
+            sds((EP, 2, HALF, D), BF), sds((EP, 8, ROWS), jnp.int32),
+            sds((4, 4, EP, 16, 256), BF), sds((4, 4, EP, 16, 512), BF),
+        ],
+        [tokens.reshape(2, HALF, D), rt, w_qkv, w_output, small],
+        [ANY] + [VM] * 4,
         [pltpu.VMEM((EP, 16, 256), BF), pltpu.VMEM((16, 512), BF)],
-        96,
+        64,
     )
-    cot_late, _ = lax.optimization_barrier((cot, xall))
-    cot_all = lax.all_gather(cot_late, "ep", axis=0)
+    cot_all = lax.all_gather(cot, "ep", axis=0)
+    w_late, xall = lax.optimization_barrier((w_qkv, xall))
+    w_full = lax.all_gather(w_late, ("dp", "ep"), axis=0, tiled=True)
 
     seq = lambda *shape: pl.BlockSpec((1, *shape), lambda s: (s,) + (0,) * len(shape))
     cut = lambda n: pl.BlockSpec((EP, 1, HALF, n), lambda s: (0, s, 0, 0))
@@ -703,7 +849,7 @@
             sds((D, D), BF),
         ],
         in_specs=[
-            cut(D), whole((DP, EP, 16, 256)), whole((DP, EP, 16, 512)), whole((LEN, 128)),
+            cut(D), whole((4, 4, EP, 16, 256)), whole((4, 4, EP, 16, 512)), whole((LEN, 128)),
             whole((LEN, 128)), seq(1, LEN),
         ],
         out_specs=[
@@ -711,7 +857,8 @@
             whole((D, D)),
         ],
         scratch_shapes=[
-            pltpu.VMEM((D, 256), BF), pltpu.VMEM((LEN, 128), BF), pltpu.VMEM((LEN, 128), BF),
+            pltpu.VMEM((D, 256), BF), pltpu.VMEM((D, 128), F32), pltpu.VMEM((LEN, 128), BF),
+            pltpu.VMEM((LEN, 128), BF),
         ],
         compiler_params=params,
     )(xall, wsl, wof, cos, sin, ids)
@@ -725,8 +872,6 @@
         24,
         [ANY, VM, VM, VM],
     )
-    w_late, moe = lax.optimization_barrier((wsl, moe))
-    w_full = lax.all_gather(w_late.reshape(D // 8, 16, 256), "ep", axis=0)
 
     each = lambda *shape: pl.BlockSpec((1, *shape), lambda j: (j,) + (0,) * len(shape))
     dw, hs, dg, du, gg, picks = pl.pallas_call(
@@ -752,36 +897,38 @@
         compiler_params=params,
     )(moe.reshape(EP, ROWS, D), cot_all, rall, gt, expert_gate, expert_up, expert_down)
 
-    dw_sum = lax.psum(dw.reshape(OWN * 3 * D, F), "dp").reshape(OWN, 3 * D, F)
-
-    part, gg_part = pl.pallas_call(
-        experts_back,
-        name="experts_back",
+    mg, gg_all, at_all, shard = pl.pallas_call(
+        experts_combine,
+        name="experts_combine",
         grid=(OWN,),
-        out_shape=[sds((EP, ROWS, 2 * D), BF), sds((EP, 8, ROWS), F32)],
+        out_shape=[
+            sds((ROWS, 2 * D), F32), sds((EP, 8, ROWS), F32), sds((EP, 2, HALF, D), BF),
+            sds((OWN, 2, 96, F), BF),
+        ],
         in_specs=[
             each(SLOTS, F), each(SLOTS, F), each(SLOTS, F), whole((OWN, SLOTS, 128)),
-            whole((EP, OWN * CAP, ROWS)), each(D, F), each(D, F), each(F, D),
-        ],
-        out_specs=[whole((EP, ROWS, 2 * D)), whole((EP, 8, ROWS))],
-        scratch_shapes=[pltpu.VMEM((EP, OWN * CAP, D), BF), pltpu.VMEM((EP, OWN * CAP, D), BF)],
-        compiler_params=params,
-    )(hs, dg, du, gg, picks, expert_gate, expert_up, expert_down)
-
-    mg, gg_all = remote_call(
-        combine, 3,
-        [sds((ROWS, 2 * D), F32), sds((EP, 8, ROWS), F32)],
-        [part, gg_part],
-        [ANY, ANY],
-        [
+            whole((EP, OWN * CAP, ROWS)), each(D, F), each(D, F), each(F, D), ANY, ANY,
+        ],
+        out_specs=[whole((ROWS, 2 * D)), ANY, ANY, whole((OWN, 2, 96, F))],
+        scratch_shapes=[
+            pltpu.VMEM((EP, OWN * CAP, D), BF), pltpu.VMEM((EP, OWN * CAP, D), BF),
+            pltpu.VMEM((EP, 8, ROWS), F32),
             pltpu.VMEM((4, ROWS, 2 * D), BF), pltpu.VMEM((4, ROWS, 2 * D), BF),
-            pltpu.VMEM((4, 2, HALF, 2 * D), BF), pltpu.VMEM((2, HALF, 2 * D), BF),
-            pltpu.VMEM((2, HALF, 2 * D), BF), pltpu.VMEM((2, HALF, 2 * D), BF),
-            pltpu.VMEM((2, HALF, 2 * D), BF),
-        ],
-        20,
-        [VM, ANY],
+            *[pltpu.VMEM((2, HALF, 2 * D), BF)] * 3,
+            *([pltpu.VMEM((2, OWN, 2, 96, F), BF)] * 4 + [pltpu.VMEM((OWN, 4, 96, F), BF)]) * 2,
+            *[pltpu.VMEM((2, OWN, 48, F), BF)] * 6,
+            pltpu.SemaphoreType.DMA((8,)),
+            pltpu.SemaphoreType.DMA((64,)),
+            pltpu.SemaphoreType.DMA((64,)),
+        ],
+        compiler_params=pltpu.CompilerParams(
+            collective_id=3, has_side_effects=True, vmem_limit_bytes=62 * MIB
+        ),
+    )(
+        hs, dg, du, gg, picks, expert_gate, expert_up, expert_down,
+        dw.reshape(OWN, 4, 4, 2, 96, F), at_own.reshape(2, HALF, D),
     )
+    dw_sum = lax.all_gather(shard.reshape(OWN, 192, F), "dp", axis=0)
 
     output, gm, gb, da, st = pl.pallas_call(
         after_experts,
@@ -795,13 +942,8 @@
         compiler_params=params,
     )(mg, gg_all, rt, moe_own, mid, cot, gt, wo)
 
-    da_all, gb_all, at_all = remote_call(
-        to_heads, 4,
-        [sds((EP, ROWS, 128), BF), sds((EP, ROWS, 128), BF), sds((EP, 2, HALF, D), BF)],
-        [da, gb, at_own.reshape(2, HALF, D)],
-        [ANY] * 3,
-        [],
-        32,
+    da_all, gb_all = remote_call(
+        to_heads, 4, [sds((EP, ROWS, 128), BF)] * 2, [da, gb], [ANY] * 2, [], 16
     )
 
     dq, dw_attn = pl.pallas_call(
@@ -831,7 +973,7 @@
     grad_x, packed = pl.pallas_call(
         first_norm_back,
         name="first_norm_back",
-        out_shape=[sds((ROWS, D), BF), sds((DP, D // DP, 512), BF)],
+        out_shape=[sds((ROWS, D), BF), sds((2, 4, 4, 64, 256), BF)],
         in_specs=[VM] * 7,
         out_specs=[VM] * 2,
         compiler_params=params,
@@ -843,15 +985,24 @@
         [packed],
         [ANY],
         [
-            pltpu.VMEM((DP, D // DP, 512), BF), pltpu.VMEM((EP, 8, 512), F32),
-            pltpu.VMEM((EP, 8, 512), F32),
+            pltpu.VMEM((4, 4, 64, 256), BF), pltpu.VMEM((4, 4, 64, 256), BF),
+            pltpu.VMEM((4, 64, 256), BF), pltpu.VMEM((4, 64, 256), BF),
+            pltpu.VMEM((4, 64, 256), BF), pltpu.VMEM((4, 64, 256), BF),
+            pltpu.VMEM((EP, 8, 512), F32), pltpu.VMEM((EP, 8, 512), F32),
         ],
         24,
         [VM] * 5,
     )
 
-    f = dw_sum.astype(F32)
-    down = jnp.concatenate([f[:, 2 * D : 2 * D + F], f[:, 2 * D + F :]], axis=2)
+    g_gate, g_up, g_down = pl.pallas_call(
+        widen,
+        name="widen",
+        grid=(OWN,),
+        out_shape=[sds((OWN, D, F), F32), sds((OWN, D, F), F32), sds((OWN, F, D), F32)],
+        in_specs=[pl.BlockSpec((DP, 1, 192, F), lambda j: (0, j, 0, 0))],
+        out_specs=[each(D, F), each(D, F), each(F, D)],
+        compiler_params=params,
+    )(dw_sum)
     return (
         output.reshape(tokens.shape),
         grad_x.reshape(tokens.shape),
@@ -862,9 +1013,9 @@
         gs[:, :EXPERTS],
         gs[:, 32],
         gs[:, 33],
-        f[:, :D],
-        f[:, D : 2 * D],
-        down,
+        g_gate,
+        g_up,
+        g_down,
     )
 
 

time: 399 us -> 367 us (0.920)
  waiting for transfers between devices: 20.1 us -> 0.72 us
  local copies, waits for them, and re-layouts: 43.8 us -> 27 us
  Pallas kernels: 314 us -> 323 us
    pallas_call x1 -> x2, Pallas kernels: 22.5 us -> 94.3 us  [the longest x1 81.9 us: per_device(): pl.pallas_call(experts_combine, name='experts_combine', grid=(OWN,), out_...]
    pallas_call x6 -> x5, Pallas kernels: 208 us -> 146 us  [remote_call(): pl.pallas_call(body, name=body.__name__, out_shape=outs, in_specs=specs,...]
    psum x1 -> x0, waiting for transfers between devices: 20 us -> none  [per_device(): dw_sum = lax.psum(dw.reshape(OWN * 3 * D, F), 'dp').reshape(OWN, 3 * D, F)]
    slice x2 -> x0, local copies, waits for them, and re-layouts: 15.3 us -> none  [the longest x1 12 us: per_device(): f[:, D:2 * D]]
    unnamed x53 -> x47, local copies, waits for them, and re-layouts: 24.9 us -> 21.9 us
  transfers between devices with their start and end apart: 3 -> 3, of which waited for: 1 -> 0; matrix products, arithmetic and copies ran while one was open for 1% -> 2% of each run, Pallas kernels for 68% -> 85%
where the time goes in v2:
time: 367 us; the launch traced here: 366 us
  Pallas kernels  323 us (88%)
  local copies, waits for them, and re-layouts  27 us (7%)
  between operations  13.9 us (4%)
    pallas_call x5, Pallas kernels, remote_call(): pl.pallas_call(body, name=body.__name__, out_shape=outs, in_specs=specs,...  146 us
    pallas_call x1, Pallas kernels, per_device(): pl.pallas_call(experts_combine, name='experts_combine', grid=(OWN,), out_...  81.9 us
    pallas_call x1, Pallas kernels, per_device(): pl.pallas_call(experts_weights, name='experts_weights', grid=(OWN,), out_...  34.1 us
    unnamed x47, local copies, waits for them, and re-layouts  21.9 us
    pallas_call x1, Pallas kernels, per_device(): pl.pallas_call(attend_back, name='attend_back', grid=(SEQS,), out_shape=[...  20.2 us
    pallas_call x1, Pallas kernels, per_device(): pl.pallas_call(project_attend, name='project_attend', grid=(SEQS,), out_s...  16.1 us
    pallas_call x1, Pallas kernels, per_device(): pl.pallas_call(widen, name='widen', grid=(OWN,), out_shape=[sds((OWN, D,...  12.4 us
  transfers between devices with their start and end apart: 3, of which 0 were waited for; matrix products, arithmetic and copies ran while one was open for 2% of the time, Pallas kernels for 85%

profile of v2, /device:TPU:1, one launch (start us, length us, event | category | flops | bytes accessed | tf_op | source)
XLA Modules:
  0.0 366.4 jit_solution(17676788950291084089)
XLA Ops:
  8.0 0.8 reshape.77
  8.7 0.8 reshape.76
  11.1 0.8 pad_maximum_fusion
  12.7 1.0 copy-done.2
  15.1 50.7 %gather_inputs.1 = (bf16[8,2,128,1024]{3,2,1,0:T(8,128)(2,1)}, s32[8,8,256]{2,1,0:T(8,128)S(1)}, bf16[4,4,8,16,256]{4,3,2,1,0:T(8,128)(2,1)S(1)}, bf16[4,4,8,16,512]{4,3,2,1,0:T(8,128)(2,1)S(1)}) custom-call(bf16[2,128,1024]{2,1,0:T(8,128)(2,1)S(1)} %copy-done.2, s32[8,256]{1,0:T(8,128)S(1)} %bitcast.32, bf16[8,2048]{1,0:T(8,128)(2,1)S(1)} %bitcast.28, ...), custom_call_target="tpu_custom_call" | custom-call | bytes 20971520 | tf_op jit(solution)/shard_map/gather_inputs/pallas_call | solution.py:121
  65.9 1.3 copy-done.5
  67.2 1.0 copy-done.7
  68.8 1.3 reshape.80.ids
  70.2 16.1 %project_attend.1 = (bf16[2,1024,128]{2,1,0:T(8,128)(2,1)}, bf16[2,1024,128]{2,1,0:T(8,128)(2,1)}, bf16[2,1024,1024]{2,1,0:T(8,128)(2,1)}, bf16[8,2,128,128]{3,2...) custom-call(bf16[8,2,128,1024]{3,2,1,0:T(8,128)(2,1)} %get-tuple-element.59.x, ...), custom_call_target="tpu_custom_call" | custom-call | tf_op jit(solution)/shard_map/project_attend/pallas_call | solution.py:842
  86.3 1.6 copy-done
  87.9 1.0 copy-done.1
  88.9 1.0 copy-done.6
  89.9 35.8 %attended_to_moe.1 = (bf16[8,2,128,1024]{3,2,1,0:T(8,128)(2,1)}, f32[256,1024]{1,0:T(8,128)S(1)}, bf16[256,1024]{1,0:T(8,128)(2,1)S(1)}, bf16[256,1024]{1,0:T(8,128)(2,1)S(1)}) custom-call(bf16[8,256,128]{2,1,0:T(8,128)(2,1)S(1)} %bitcast.23, bf16[256,1024]{1,0:T(8,128)(2,1)S(1)} %bitcast.22, bf16[1024,1024]{1,0:T(8,128)(2,1)S(1)} %copy-done, ...), custom_call_target="tpu_custom_call" | custom-call | bytes 20971520 | tf_op jit(solution)/shard_map/attended_to_moe/pallas_call | solution.py:121
  125.8 1.0 copy-done.10
  126.7 0.8 copy-done.11
  127.5 0.8 copy-done.16
  128.3 34.1 %experts_weights.1 = (bf16[4,3072,512]{2,1,0:T(8,128)(2,1)}, bf16[4,640,512]{2,1,0:T(8,128)(2,1)}, bf16[4,640,512]{2,1,0:T(8,128)(2,1)}, bf16[4,640,512]{2,1,0:T...) custom-call(bf16[8,256,1024]{2,1,0:T(8,128)(2,1)} %bitcast.34, ...), custom_call_target="tpu_custom_call" | custom-call | tf_op jit(solution)/shard_map/experts_weights/pallas_call | solution.py:877
  162.4 81.9 %experts_combine.1 = (f32[256,2048]{1,0:T(8,128)}, f32[8,8,256]{2,1,0:T(8,128)}, bf16[8,2,128,1024]{3,2,1,0:T(8,128)(2,1)}, bf16[4,2,96,512]{3,2,1,0:T(8,128)(2,1)}) custom-call(bf16[4,640,512]{2,1,0:T(8,128)(2,1)} %get-tuple-element.67.hs, bf16[4,640,512]{2,1,0:T(8,128)(2,1)} %get-tuple-element.68.dg, bf16[4,640,512]{2,1,0:T(8,128)(2,1)} %get-tuple-element.69.du, ...), custom_call_target="tpu_custom_call" | custom-call | tf_op jit(solution)/shard_map/experts_combine/pallas_call | solution.py:900
  244.3 5.9 %after_experts.1 = (bf16[256,1024]{1,0:T(8,128)(2,1)}, f32[256,1024]{1,0:T(8,128)}, bf16[8,256,128]{2,1,0:T(8,128)(2,1)}, bf16[8,256,128]{2,1,0:T(8,128)(2,1)}, f32[128,1024]{1,0:T(8,128)}) custom-call(f32[256,2048]{1,0:T(8,128)} %get-tuple-element.74.mg, f32[8,8,256]{2,1,0:T(8,128)} %get-tuple-element.75.gg, s32[8,256]{1,0:T(8,128)} %bitcast.31, ...), custom_call_target="tpu_custom_call" | custom-call | tf_op jit(solution)/shard_map/after_experts/pallas_call | solution.py:933
  250.3 1.1 copy-done.14
  251.3 1.1 copy-done.15
  252.4 15.8 %to_heads.1 = (bf16[8,256,128]{2,1,0:T(8,128)(2,1)S(1)}, bf16[8,256,128]{2,1,0:T(8,128)(2,1)S(1)}) custom-call(bf16[8,256,128]{2,1,0:T(8,128)(2,1)S(1)} %copy-done.15, bf16[8,256,128]{2,1,0:T(8,128)(2,1)S(1)} %copy-done.14), custom_call_target="tpu_custom_call" | custom-call | bytes 20971520 | tf_op jit(solution)/shard_map/to_heads/pallas_call | solution.py:121
  268.2 0.8 copy-done.12
  269.0 0.8 copy-done.13
  269.8 20.2 %attend_back.1 = (bf16[8,2,128,256]{3,2,1,0:T(8,128)(2,1)}, f32[1024,384]{1,0:T(8,128)}) custom-call(bf16[2,1024,128]{2,1,0:T(8,128)(2,1)} %get-tuple-element.79.q, bf16[2,1024,128]{2,1,0:T(8,128)(2,1)} %get-tuple-element.80.kv, bf16[2,1024,1024]{2,1,0:T(8,128)(2,1)} %get-tuple-element.81.nrm, bf16[8,2,128,128]{3,2,1,0:T(8,128)(2,1)} %get-tuple-element.62.att, ...), custom_call_target="tpu_custom_call" | custom-call | tf_op jit(solution)/shard_map/attend_back/pallas_call | solution.py:949
  290.0 1.3 copy-done.8
  291.3 15.8 %to_tokens.1.dq = bf16[8,256,256]{2,1,0:T(8,128)(2,1)S(1)} custom-call(bf16[8,256,256]{2,1,0:T(8,128)(2,1)S(1)} %bitcast.24), custom_call_target="tpu_custom_call" | custom-call | bytes 20971520 | tf_op jit(solution)/shard_map/to_tokens/pallas_call | solution.py:121
  307.2 1.0 copy-done.4
  308.1 6.6 %first_norm_back.1 = (bf16[256,1024]{1,0:T(8,128)(2,1)}, bf16[2,4,4,64,256]{4,3,2,1,0:T(8,128)(2,1)}) custom-call(bf16[8,256,256]{2,1,0:T(8,128)(2,1)} %copy-done.4, bf16[1024,2048]{1,0:T(8,128)(2,1)} %all-gather.6.cloned.1.call-done.wf, bf16[256,1024]{1,0:T(8,128)(2,1)} %bitcast.21, f32[256,1024]{1,0:T(8,128)} %get-tuple-element.90.gm, ...), custom_call_target="tpu_custom_call" | custom-call | tf_op jit(solution)/shard_map/first_norm_back/pallas_call | solution.py:973
  314.7 1.2 copy-done.9
  316.0 27.7 %sum_weights.1 = (f32[8,1024]{1,0:T(8,128)S(1)}, f32[8,512]{1,0:T(8,128)S(1)}, f32[8,512]{1,0:T(8,128)S(1)}, f32[8,1024]{1,0:T(8,128)S(1)}, f32[8,128]{1,0:T(8,128)S(1)}) custom-call(bf16[2,4,4,64,256]{4,3,2,1,0:T(8,128)(2,1)S(1)} %copy-done.9), custom_call_target="tpu_custom_call" | custom-call | bytes 20971520 | tf_op jit(solution)/shard_map/sum_weights/pallas_call | solution.py:121
  344.4 12.4 %widen.1 = (f32[4,1024,512]{2,1,0:T(8,128)}, f32[4,1024,512]{2,1,0:T(8,128)}, f32[4,512,1024]{2,1,0:T(8,128)}) custom-call(bf16[16,4,192,512]{3,2,1,0:T(8,128)(2,1)} %all-gather.8.cloned.1.call-done.dw), custom_call_target="tpu_custom_call" | custom-call | tf_op jit(solution)/shard_map/widen/pallas_call | solution.py:997
  (48 shorter events, 9.0 us)
Async XLA Ops:
  7.2 121.1 %all-gather.4.cloned.1.call-start = ((), (), s32[]{:S(2)}) async-start(), calls=%async_computation | async-start | bytes 4718592 | tf_op jit(solution)/shard_map/all_gather | solution.py:836
  7.9 300.2 %all-gather.6.cloned.1.call-start = ((), (), s32[]{:S(2)}) async-start(), calls=%async_computation.1 | async-start | bytes 4227072 | tf_op jit(solution)/shard_map/all_gather | solution.py:838
  11.9 56.9 %copy-start.17 = (bf16[8,8,256]{2,0,1:T(8,128)(2,1)}, bf16[8,8,256]{2,0,1:T(8,128)(2,1)S(1)}, u32[]{:S(2)}) copy-start(bf16[8,8,256]{2,0,1:T(8,128)(2,1)S(1)} %pad_maximum_fusion) | copy-start | bytes 98308
  12.7 1.0 copy-start.2
  13.7 0.7 copy-start.19
  14.4 0.7 copy-start.20
  65.9 1.3 copy-start.5
  67.2 1.0 copy-start.7
  68.2 0.6 copy-start.18
  68.8 275.6 %all-gather.8.cloned.1.call-start = ((), (), s32[]{:S(2)}) async-start(), calls=%async_computation.2 | async-start | bytes 13369344 | tf_op jit(solution)/shard_map/all_gather | solution.py:931
  70.2 16.1 %copy-start.3 = (bf16[2,128,1024]{2,1,0:T(8,128)(2,1)S(1)}, bf16[2,128,1024]{2,1,0:T(8,128)(2,1)}, u32[]{:S(2)}) copy-start(bf16[2,128,1024]{2,1,0:T(8,128)(2,1)} %x.1) | copy-start | bytes 1572868
  86.3 1.6 copy-start
  87.9 1.0 copy-start.1
  88.9 1.0 copy-start.6
  125.8 1.0 copy-start.10
  126.7 0.8 copy-start.11
  127.5 0.8 copy-start.16
  250.2 1.1 copy-start.14
  251.3 1.1 copy-start.15
  268.2 0.8 copy-start.12
  269.0 0.8 copy-start.13
  290.0 1.3 copy-start.8
  307.2 1.0 copy-start.4
  314.7 1.2 copy-start.9
Sparse Core Ops, SparseCore 0:
  9.7 52.6 all-gather.3
  68.9 66.3 all-gather.5
  244.4 94.3 all-gather.7
